TPU v7x, 32 devices: a whole 2x2x4 slice. The times are simulated.
32 devices in a mesh: dp: 16 (over z, y, core), tensor: 2 (over x).
Axes of the slice: x: 2, y: 2, z: 4, core: 2. Of those that a mesh axis runs over, the one named last changes fastest.
Arguments:
- frames: bfloat16 [65536, 512], P('dp'), may hold values from -6 to 6
- context_keys: bfloat16 [128, 10, 512], P('dp', None, 'tensor'), may hold values from -6 to 6
- context_values: bfloat16 [128, 10, 512], P('dp', None, 'tensor'), may hold values from -6 to 6
- time_start: int32 [128], P('dp'), may hold values from 0 to 511
- time_width: int32 [128], P('dp'), may hold values from 0 to 40
- freq_start: int32 [128], P('dp'), may hold values from 0 to 511
- freq_width: int32 [128], P('dp'), may hold values from 0 to 64
- context_count: int32 [128], P('dp'), may hold values from 0 to 10
- gain_one: float32 [512], replicated, may hold values from 0.5 to 1.5
- shift_one: float32 [512], replicated, may hold values from -1.75 to 1.75
- query_w: bfloat16 [512, 512], P('dp', 'tensor'), may hold values from -0.25 to 0.25
- key_w: bfloat16 [512, 512], P('dp', 'tensor'), may hold values from -0.25 to 0.25
- value_w: bfloat16 [512, 512], P('dp', 'tensor'), may hold values from -0.25 to 0.25
- out_w: bfloat16 [512, 512], P('tensor', 'dp'), may hold values from -0.75 to 0.75
- gain_two: float32 [512], replicated, may hold values from 0.5 to 1.5
- shift_two: float32 [512], replicated, may hold values from -1.75 to 1.75
- inner_w: bfloat16 [512, 2048], P('dp', 'tensor'), may hold values from -0.25 to 0.25
- inner_b: float32 [2048], P('tensor'), may hold values from -3 to 3
- outer_w: bfloat16 [2048, 512], P('tensor', 'dp'), may hold values from -0.1875 to 0.1875
- outer_b: float32 [512], replicated, may hold values from -3 to 3
- cotangent: bfloat16 [65536, 512], P('dp'), may hold values from -6 to 6
Outputs:
- output: bfloat16 [65536, 512], P('dp')
- grad_frames: bfloat16 [65536, 512], P('dp')
- grad_context_keys: float32 [128, 10, 512], P('dp', None, 'tensor')
- grad_context_values: float32 [128, 10, 512], P('dp', None, 'tensor')
- grad_gain_one: float32 [512], P('dp')
- grad_shift_one: float32 [512], P('dp')
- grad_query_w: float32 [512, 512], P('dp', 'tensor')
- grad_key_w: float32 [512, 512], P('dp', 'tensor')
- grad_value_w: float32 [512, 512], P('dp', 'tensor')
- grad_out_w: float32 [512, 512], P('tensor', 'dp')
- grad_gain_two: float32 [512], P('dp')
- grad_shift_two: float32 [512], P('dp')
- grad_inner_w: float32 [512, 2048], P('dp', 'tensor')
- grad_inner_b: float32 [2048], P(('tensor', 'dp'))
- grad_outer_w: float32 [2048, 512], P('tensor', 'dp')
- grad_outer_b: float32 [512], P('dp')
All inputs are finite; a program needn't handle non-finite values.
Results may differ from a plain program's by a relative error of at most 0.024.
Values may be sent and summed in bfloat16 or wider, within the bound.
No kernel may reach another device: no remote copies, remote signals or barrier semaphores. Data moves between devices by JAX's collectives and lax.ppermute only.
A program may use at most 192 MiB of HBM per device.

v0:
```python
import jax
import jax.numpy as jnp
from jax import lax
from jax.sharding import PartitionSpec as P

D = 512
HEAD_DIM = 64
SPAN = 512
LEFT = 10
RIGHT = 2


epsilon = 1e-05


def layer_norm(values, gain_row, shift_row):
    center = values - jnp.mean(values, axis=-1, keepdims=True)
    variance = jnp.mean(center * center, axis=-1, keepdims=True)
    return center * lax.rsqrt(variance + epsilon) * gain_row + shift_row


def gelu_tanh(values):
    return (
        0.5
        * values
        * (1.0 + jnp.tanh(0.7978845608 * (values + 0.044715 * values * values * values)))
    )


def keep_masks(time_start, time_width, freq_start, freq_width):
    positions = jnp.arange(SPAN)[None, :]
    hidden_time = (positions >= time_start[:, None]) & (
        positions < time_start[:, None] + time_width[:, None]
    )
    columns = jnp.arange(D)[None, :]
    hidden_freq = (columns >= freq_start[:, None]) & (
        columns < freq_start[:, None] + freq_width[:, None]
    )
    keep_time = jnp.where(hidden_time, 0.0, 1.0).astype(jnp.float32)
    keep_freq = jnp.where(hidden_freq, 0.0, 1.0).astype(jnp.float32)
    return (keep_time, keep_freq)


def window_mask(context_count):
    query_block = min(128, SPAN)
    blocks = SPAN // query_block
    window = query_block + LEFT + RIGHT
    query_place = jnp.arange(query_block)[None, :, None]
    key_place = jnp.arange(window)[None, None, :]
    block_start = jnp.arange(blocks)[:, None, None] * query_block
    places = block_start + key_place - LEFT
    allowed = (key_place >= query_place) & (key_place <= query_place + LEFT + RIGHT)
    return allowed & (places >= -context_count) & (places < SPAN)


def windows(rows_all):
    query_block = min(128, SPAN)
    blocks = SPAN // query_block
    window = query_block + LEFT + RIGHT
    padded = jnp.concatenate(
        [rows_all, jnp.zeros((RIGHT,) + rows_all.shape[1:], rows_all.dtype)], axis=0
    )
    return jnp.stack(
        [padded[number * query_block : number * query_block + window] for number in range(blocks)],
        axis=0,
    )


def unwindow(tiles):
    query_block = min(128, SPAN)
    window = tiles.shape[1]
    summed = jnp.zeros((SPAN + LEFT + RIGHT,) + tiles.shape[2:], jnp.float32)
    for number in range(tiles.shape[0]):
        summed = summed.at[number * query_block : number * query_block + window].add(tiles[number])
    return summed[: LEFT + SPAN]


def attend_span(pieces):
    query_rows, key_rows, value_rows, context_count = pieces
    heads = query_rows.shape[1]
    query_block = min(128, SPAN)
    blocks = SPAN // query_block
    query_tiles = query_rows.reshape(blocks, query_block, heads, HEAD_DIM)
    key_tiles = windows(key_rows)
    value_tiles = windows(value_rows)
    scores = jnp.einsum(
        "bqhe,bkhe->hbqk", query_tiles, key_tiles, preferred_element_type=jnp.float32
    ) * HEAD_DIM ** (-0.5)
    scores = jnp.where(window_mask(context_count)[None], scores, -1e30)
    row_top = jnp.max(scores, axis=-1, keepdims=True)
    row_total = jnp.sum(jnp.exp(scores - row_top), axis=-1, keepdims=True)
    log_total = row_top + jnp.log(row_total)
    probs_low = jnp.exp(scores - log_total).astype(jnp.bfloat16)
    attended = jnp.einsum(
        "hbqk,bkhe->bqhe", probs_low, value_tiles, preferred_element_type=jnp.float32
    )
    return (attended.reshape(SPAN, heads, HEAD_DIM), log_total[..., 0])


def attend_back(pieces):
    query_rows, key_rows, value_rows, context_count, log_total, grad_rows = pieces
    heads = query_rows.shape[1]
    query_block = min(128, SPAN)
    blocks = SPAN // query_block
    score_scale = HEAD_DIM ** (-0.5)
    query_tiles = query_rows.reshape(blocks, query_block, heads, HEAD_DIM)
    grad_tiles = grad_rows.reshape(blocks, query_block, heads, HEAD_DIM)
    key_tiles = windows(key_rows)
    value_tiles = windows(value_rows)
    scores = (
        jnp.einsum("bqhe,bkhe->hbqk", query_tiles, key_tiles, preferred_element_type=jnp.float32)
        * score_scale
    )
    probs = jnp.where(window_mask(context_count)[None], jnp.exp(scores - log_total[..., None]), 0.0)
    grad_value_tiles = jnp.einsum(
        "hbqk,bqhe->bkhe",
        probs.astype(jnp.bfloat16),
        grad_tiles,
        preferred_element_type=jnp.float32,
    )
    grad_probs = jnp.einsum(
        "bqhe,bkhe->hbqk", grad_tiles, value_tiles, preferred_element_type=jnp.float32
    )
    row_delta = jnp.sum(probs * grad_probs, axis=-1, keepdims=True)
    grad_scores = (probs * (grad_probs - row_delta)).astype(jnp.bfloat16)
    grad_queries = (
        jnp.einsum("hbqk,bkhe->bqhe", grad_scores, key_tiles, preferred_element_type=jnp.float32)
        * score_scale
    )
    grad_key_tiles = (
        jnp.einsum("hbqk,bqhe->bkhe", grad_scores, query_tiles, preferred_element_type=jnp.float32)
        * score_scale
    )
    return (
        grad_queries.reshape(SPAN, heads, HEAD_DIM),
        unwindow(grad_key_tiles),
        unwindow(grad_value_tiles),
    )


def attention_forward(queries, keys_new, values_new, context_keys, context_values, context_count):
    spans = context_count.shape[0]
    width = queries.shape[1]
    heads = width // HEAD_DIM
    query_blocks = queries.reshape(spans, SPAN, heads, HEAD_DIM)
    key_blocks = jnp.concatenate(
        [
            context_keys.reshape(spans, LEFT, heads, HEAD_DIM),
            keys_new.reshape(spans, SPAN, heads, HEAD_DIM),
        ],
        axis=1,
    )
    value_blocks = jnp.concatenate(
        [
            context_values.reshape(spans, LEFT, heads, HEAD_DIM),
            values_new.reshape(spans, SPAN, heads, HEAD_DIM),
        ],
        axis=1,
    )
    attended, log_totals = lax.map(
        attend_span, (query_blocks, key_blocks, value_blocks, context_count)
    )
    return (
        attended.reshape(spans * SPAN, width).astype(jnp.bfloat16),
        (query_blocks, key_blocks, value_blocks, log_totals),
    )


def attention_backward(kept, context_count, grad_attended):
    query_blocks, key_blocks, value_blocks, log_totals = kept
    spans, heads = (query_blocks.shape[0], query_blocks.shape[2])
    width = heads * HEAD_DIM
    grad_blocks = grad_attended.reshape(spans, SPAN, heads, HEAD_DIM)
    grad_q, grad_k, grad_v = lax.map(
        attend_back,
        (query_blocks, key_blocks, value_blocks, context_count, log_totals, grad_blocks),
    )
    context_key_grad = grad_k[:, :LEFT].reshape(spans, LEFT, width)
    context_value_grad = grad_v[:, :LEFT].reshape(spans, LEFT, width)
    grad_queries = grad_q.reshape(spans * SPAN, width).astype(jnp.bfloat16)
    grad_keys = grad_k[:, LEFT:].reshape(spans * SPAN, width).astype(jnp.bfloat16)
    grad_values = grad_v[:, LEFT:].reshape(spans * SPAN, width).astype(jnp.bfloat16)
    return (context_key_grad, context_value_grad, grad_queries, grad_keys, grad_values)


def share_rows(array):
    rows = array.shape[0] // lax.axis_size("tensor")
    return lax.dynamic_slice_in_dim(array, lax.axis_index("tensor") * rows, rows, 0)


def body(
    frames,
    context_keys,
    context_values,
    time_start,
    time_width,
    freq_start,
    freq_width,
    context_count,
    gain_one,
    shift_one,
    query_w,
    key_w,
    value_w,
    out_w,
    gain_two,
    shift_two,
    inner_w,
    inner_b,
    outer_w,
    outer_b,
    cotangent,
):
    query_full, key_full, value_full, out_full, inner_full, outer_full = (
        lax.all_gather(query_w, "dp", axis=0, tiled=True),
        lax.all_gather(key_w, "dp", axis=0, tiled=True),
        lax.all_gather(value_w, "dp", axis=0, tiled=True),
        lax.all_gather(out_w, "dp", axis=1, tiled=True),
        lax.all_gather(inner_w, "dp", axis=0, tiled=True),
        lax.all_gather(outer_w, "dp", axis=1, tiled=True),
    )
    spans = time_start.shape[0]
    total_rows = spans * SPAN
    keep_time, keep_freq = keep_masks(time_start, time_width, freq_start, freq_width)
    keep_full = (keep_time[:, :, None] * keep_freq[:, None, :]).reshape(total_rows, D)
    masked = frames.astype(jnp.float32) * keep_full
    normed_one = layer_norm(masked, gain_one, shift_one).astype(jnp.bfloat16)
    queries = jnp.dot(normed_one, query_full, preferred_element_type=jnp.float32).astype(
        jnp.bfloat16
    )
    keys_new = jnp.dot(normed_one, key_full, preferred_element_type=jnp.float32).astype(
        jnp.bfloat16
    )
    values_new = jnp.dot(normed_one, value_full, preferred_element_type=jnp.float32).astype(
        jnp.bfloat16
    )
    attended, kept = attention_forward(
        queries, keys_new, values_new, context_keys, context_values, context_count
    )
    head_part = (
        jnp.dot(attended, out_full, preferred_element_type=jnp.float32)
        .astype(jnp.bfloat16)
        .astype(jnp.float32)
    )
    middle = masked + lax.psum(head_part.astype(jnp.bfloat16), "tensor").astype(jnp.float32)
    normed_two = layer_norm(middle, gain_two, shift_two).astype(jnp.bfloat16)
    inner_act = jnp.dot(normed_two, inner_full, preferred_element_type=jnp.float32) + inner_b
    hidden = gelu_tanh(inner_act).astype(jnp.bfloat16)
    unit_part = (
        jnp.dot(hidden, outer_full, preferred_element_type=jnp.float32)
        .astype(jnp.bfloat16)
        .astype(jnp.float32)
    )
    output = (
        middle + lax.psum(unit_part.astype(jnp.bfloat16), "tensor").astype(jnp.float32) + outer_b
    ).astype(jnp.bfloat16)
    query_back, key_back, value_back, out_back, inner_back, outer_back = (
        lax.all_gather(query_w, "dp", axis=0, tiled=True),
        lax.all_gather(key_w, "dp", axis=0, tiled=True),
        lax.all_gather(value_w, "dp", axis=0, tiled=True),
        lax.all_gather(out_w, "dp", axis=1, tiled=True),
        lax.all_gather(inner_w, "dp", axis=0, tiled=True),
        lax.all_gather(outer_w, "dp", axis=1, tiled=True),
    )
    upstream = cotangent.astype(jnp.float32)
    grad_outer_w = jnp.dot(hidden.T, cotangent, preferred_element_type=jnp.float32)
    grad_hidden = jnp.dot(cotangent, outer_back.T, preferred_element_type=jnp.float32)
    gelu_pull = jax.vjp(gelu_tanh, inner_act)[1]
    grad_inner = gelu_pull(grad_hidden)[0].astype(jnp.bfloat16)
    grad_inner_w = jnp.dot(normed_two.T, grad_inner, preferred_element_type=jnp.float32)
    grad_inner_b = jnp.sum(grad_inner, axis=0, dtype=jnp.float32)
    second_share = lax.psum_scatter(
        jnp.dot(grad_inner, inner_back.T, preferred_element_type=jnp.float32).astype(jnp.bfloat16),
        "tensor",
        scatter_dimension=0,
        tiled=True,
    ).astype(jnp.float32)
    upstream_share = share_rows(upstream)
    second_pull = jax.vjp(layer_norm, share_rows(middle), gain_two, shift_two)[1]
    grad_mid_norm, grad_gain_two, grad_shift_two = second_pull(second_share)
    grad_outer_b = jnp.sum(upstream_share, axis=0)
    grad_middle = lax.all_gather(
        (upstream_share + grad_mid_norm).astype(jnp.bfloat16), "tensor", axis=0, tiled=True
    ).astype(jnp.float32)
    grad_middle_low = grad_middle.astype(jnp.bfloat16)
    grad_out_w = jnp.dot(attended.T, grad_middle_low, preferred_element_type=jnp.float32)
    grad_attended = jnp.dot(grad_middle_low, out_back.T, preferred_element_type=jnp.float32).astype(
        jnp.bfloat16
    )
    grad_context_keys, grad_context_values, grad_queries, grad_keys, grad_values = (
        attention_backward(kept, context_count, grad_attended)
    )
    grad_query_w = jnp.dot(normed_one.T, grad_queries, preferred_element_type=jnp.float32)
    grad_key_w = jnp.dot(normed_one.T, grad_keys, preferred_element_type=jnp.float32)
    grad_value_w = jnp.dot(normed_one.T, grad_values, preferred_element_type=jnp.float32)
    query_term = jnp.dot(grad_queries, query_back.T, preferred_element_type=jnp.float32)
    key_term = jnp.dot(grad_keys, key_back.T, preferred_element_type=jnp.float32)
    value_term = jnp.dot(grad_values, value_back.T, preferred_element_type=jnp.float32)
    first_share = lax.psum_scatter(
        (query_term + key_term + value_term).astype(jnp.bfloat16),
        "tensor",
        scatter_dimension=0,
        tiled=True,
    ).astype(jnp.float32)
    first_pull = jax.vjp(layer_norm, share_rows(masked), gain_one, shift_one)[1]
    grad_mask_norm, grad_gain_one, grad_shift_one = first_pull(first_share)
    frames_share = ((share_rows(grad_middle) + grad_mask_norm) * share_rows(keep_full)).astype(
        jnp.bfloat16
    )
    grad_frames = lax.all_gather(frames_share, "tensor", axis=0, tiled=True)
    grad_gain_one, grad_shift_one, grad_gain_two, grad_shift_two, grad_outer_b = lax.psum(
        (grad_gain_one, grad_shift_one, grad_gain_two, grad_shift_two, grad_outer_b), "tensor"
    )
    summed = (
        lax.psum_scatter(
            grad_query_w.astype(jnp.bfloat16), "dp", scatter_dimension=0, tiled=True
        ).astype(jnp.float32),
        lax.psum_scatter(
            grad_key_w.astype(jnp.bfloat16), "dp", scatter_dimension=0, tiled=True
        ).astype(jnp.float32),
        lax.psum_scatter(
            grad_value_w.astype(jnp.bfloat16), "dp", scatter_dimension=0, tiled=True
        ).astype(jnp.float32),
        lax.psum_scatter(
            grad_out_w.astype(jnp.bfloat16), "dp", scatter_dimension=1, tiled=True
        ).astype(jnp.float32),
        lax.psum_scatter(
            grad_inner_w.astype(jnp.bfloat16), "dp", scatter_dimension=0, tiled=True
        ).astype(jnp.float32),
        lax.psum_scatter(
            grad_outer_w.astype(jnp.bfloat16), "dp", scatter_dimension=1, tiled=True
        ).astype(jnp.float32),
        lax.psum_scatter(
            grad_inner_b.astype(jnp.bfloat16), "dp", scatter_dimension=0, tiled=True
        ).astype(jnp.float32),
        lax.psum_scatter(
            grad_gain_one.astype(jnp.bfloat16), "dp", scatter_dimension=0, tiled=True
        ).astype(jnp.float32),
        lax.psum_scatter(
            grad_shift_one.astype(jnp.bfloat16), "dp", scatter_dimension=0, tiled=True
        ).astype(jnp.float32),
        lax.psum_scatter(
            grad_gain_two.astype(jnp.bfloat16), "dp", scatter_dimension=0, tiled=True
        ).astype(jnp.float32),
        lax.psum_scatter(
            grad_shift_two.astype(jnp.bfloat16), "dp", scatter_dimension=0, tiled=True
        ).astype(jnp.float32),
        lax.psum_scatter(
            grad_outer_b.astype(jnp.bfloat16), "dp", scatter_dimension=0, tiled=True
        ).astype(jnp.float32),
    )
    (
        sum_query,
        sum_key,
        sum_value,
        sum_out,
        sum_inner,
        sum_outer,
        sum_inner_b,
        sum_gain_one,
        sum_shift_one,
        sum_gain_two,
        sum_shift_two,
        sum_outer_b,
    ) = summed
    return (
        output,
        grad_frames,
        grad_context_keys,
        grad_context_values,
        sum_gain_one,
        sum_shift_one,
        sum_query,
        sum_key,
        sum_value,
        sum_out,
        sum_gain_two,
        sum_shift_two,
        sum_inner,
        sum_inner_b,
        sum_outer,
        sum_outer_b,
    )


def solution(mesh):
    in_specs = (
        P("dp", None),
        P("dp", None, "tensor"),
        P("dp", None, "tensor"),
        P("dp"),
        P("dp"),
        P("dp"),
        P("dp"),
        P("dp"),
        P(),
        P(),
        P("dp", "tensor"),
        P("dp", "tensor"),
        P("dp", "tensor"),
        P("tensor", "dp"),
        P(),
        P(),
        P("dp", "tensor"),
        P("tensor"),
        P("tensor", "dp"),
        P(),
        P("dp", None),
    )
    out_specs = (
        P("dp", None),
        P("dp", None),
        P("dp", None, "tensor"),
        P("dp", None, "tensor"),
        P("dp"),
        P("dp"),
        P("dp", "tensor"),
        P("dp", "tensor"),
        P("dp", "tensor"),
        P("tensor", "dp"),
        P("dp"),
        P("dp"),
        P("dp", "tensor"),
        P(("tensor", "dp")),
        P("tensor", "dp"),
        P("dp"),
    )
    return jax.shard_map(body, mesh=mesh, in_specs=in_specs, out_specs=out_specs, check_vma=False)
```

profile of v0, /device:TPU:0, one launch (start us, length us, event | category | flops | bytes accessed | tf_op | source)
XLA Modules:
  0.0 1336.4 jit_solution(6470065615775718115)
XLA Ops:
  10.9 8.4 convert_multiply_fusion
  22.3 23.8 %all_gather.30 = bf16[512,256]{1,0:T(8,128)(2,1)S(1)} all-gather(bf16[32,256]{1,0:T(8,128)(2,1)S(1)} %copy-done.35), channel_id=1, replica_groups=mesh['dp'=16,'tensor'=2] {'dp'}, dimensions={0}, use_global_device_ids=true | all-gather | bytes 278528 | tf_op jit(solution)/shard_map/all_gather | solution.py:217
  63.7 18.6 %all_gather.32 = bf16[512,256]{1,0:T(8,128)(2,1)S(1)} all-gather(bf16[32,256]{1,0:T(8,128)(2,1)S(1)} %copy-done.36), channel_id=1, replica_groups=mesh['dp'=16,'tensor'=2] {'dp'}, dimensions={0}, use_global_device_ids=true | all-gather | bytes 278528 | tf_op jit(solution)/shard_map/all_gather | solution.py:216
  98.9 19.5 %all_gather.31 = bf16[512,256]{1,0:T(8,128)(2,1)S(1)} all-gather(bf16[32,256]{1,0:T(8,128)(2,1)S(1)} %copy-done.37), channel_id=1, replica_groups=mesh['dp'=16,'tensor'=2] {'dp'}, dimensions={0}, use_global_device_ids=true | all-gather | bytes 278528 | tf_op jit(solution)/shard_map/all_gather | solution.py:215
  137.2 99.9 %while.39 = (s32[]{:T(128)}, bf16[8,512,4,64]{1,3,2,0:T(8,128)(2,1)}, f32[8,4,4,128]{3,2,1,0:T(4,128)}, bf16[8,522,4,64]{1,3,2,0:T(8,128)(2,1)}, s32[8]{0:T(128)...) while((s32[]{:T(128)}, ...), condition=%wide.region_5.6_spmd, body=%wide.region_2.5_spmd.sunk | while | flops 76464968 | bytes 10016161 | solution.py:160
  240.8 18.2 %all_gather.33 = bf16[256,512]{0,1:T(8,128)(2,1)S(1)} all-gather(bf16[256,32]{0,1:T(8,128)(2,1)S(1)} %copy-done.38), channel_id=1, replica_groups=mesh['dp'=16,'tensor'=2] {'dp'}, dimensions={1}, use_global_device_ids=true | all-gather | bytes 278528 | tf_op jit(solution)/shard_map/all_gather | solution.py:218
  263.7 105.1 %all-reduce.17.cloned.1.call-done = bf16[4096,512]{1,0:T(8,128)(2,1)} async-done(((bf16[4096,512]{1,0:T(8,128)(2,1)}), bf16[4096,512]{1,0:T(8,128)(2,1)}) %all-reduce.17.cloned.1.call-update) | async-done | bytes 4194320 | tf_op jit(solution)/shard_map/psum | solution.py:245
  377.2 15.6 %multiply_convert_fusion.1 = (bf16[4096,1024]{1,0:T(8,128)(2,1)}, f32[4096,1024]{1,0:T(8,128)}) fusion(f32[1024]{0:T(1024)S(1)} %copy-done.47, bf16[512,1024]{1,0:T(8,128)(2,1)} %all-gather.5.cloned.1.call-done, f32[4096,512]{1,0:T(8,128)} %copy-done, f32[512]{0:T(512)S(1)} %copy-done.48, f32[512]{0:T(512)S(1)} %copy-done.41, f32[4096]{0:T(1024)S(1)} %add_rsqrt_fusion, ...), kind=kOutput, calls=%fused_computation.134 | convolution fusion | flops 4347396096 | bytes 34643968 | tf_op jit(solution)/shard_map/dot_general | solution.py:247
  392.8 21.4 %fusion.86 = (bf16[1024]{0:T(1024)(128)(2,1)}, bf16[4096,1024]{1,0:T(8,128)(2,1)S(1)}) fusion(f32[4096,1024]{1,0:T(8,128)} %get-tuple-element.529, f32[1024]{0:T(1024)S(1)} %copy-done.47, bf16[4096,512]{1,0:T(8,128)(2,1)} %param.61, bf16[1024,512]{0,1:T(8,128)(2,1)} %all-gather.7.cloned.1.call-done), kind=kOutput, calls=%fused_computation.218 | convolution fusion | flops 4404018176 | bytes 30414848 | tf_op jit(solution)/shard_map/dot_general | solution.py:267
  429.5 48.9 %reduce-scatter.9.cloned.1.call-done = bf16[2048,512]{1,0:T(8,128)(2,1)} async-done(((bf16[4096,512]{1,0:T(8,128)(2,1)}), bf16[2048,512]{1,0:T(8,128)(2,1)}) %reduce-scatter.9.cloned.1.call-update) | async-done | bytes 2097168 | tf_op jit(solution)/shard_map/reduce_scatter | solution.py:272
  490.4 54.5 %all-gather.9.cloned.1.call-done = bf16[4096,512]{1,0:T(8,128)(2,1)} async-done(((bf16[2048,512]{1,0:T(8,128)(2,1)}), bf16[4096,512]{1,0:T(8,128)(2,1)}) %all-gather.9.cloned.1.call-update) | async-done | bytes 4194320 | tf_op jit(solution)/shard_map/all_gather | solution.py:282
  560.0 167.3 %while.40 = (s32[]{:T(128)}, bf16[8,512,4,64]{1,3,2,0:T(8,128)(2,1)}, f32[8,522,4,64]{1,3,2,0:T(8,128)}, f32[8,522,4,64]{1,3,2,0:T(8,128)}, bf16[8,522,4,64]{1,3...) while((s32[]{:T(128)}, ...), condition=%wide.region_17.18_spmd, body=%wide.region_15.17_spmd.sunk | while | flops 189049664 | bytes 30121624 | solution.py:174
  748.8 11.7 convolution_convert_fusion.8
  760.6 10.4 convolution_convert_fusion.7
  771.2 9.5 convolution_convert_fusion.1
  818.2 45.7 %reduce-scatter.21.cloned.1.call-done = bf16[32,1024]{1,0:T(8,128)(2,1)} async-done(((bf16[512,1024]{1,0:T(8,128)(2,1)}), bf16[32,1024]{1,0:T(8,128)(2,1)}) %reduce-scatter.21.cloned.1.call-update) | async-done | bytes 65552 | tf_op jit(solution)/shard_map/reduce_scatter | solution.py:327
  865.4 58.4 %reduce-scatter.23.cloned.1.call-done = bf16[1024,32]{0,1:T(8,128)(2,1)} async-done(((bf16[1024,512]{0,1:T(8,128)(2,1)}), bf16[1024,32]{0,1:T(8,128)(2,1)}) %reduce-scatter.23.cloned.1.call-update) | async-done | bytes 65552 | tf_op jit(solution)/shard_map/reduce_scatter | solution.py:330
  925.3 108.6 %all-reduce.19.cloned.1.call-done = bf16[4096,512]{1,0:T(8,128)(2,1)} async-done(((bf16[4096,512]{1,0:T(8,128)(2,1)}), bf16[4096,512]{1,0:T(8,128)(2,1)}) %all-reduce.19.cloned.1.call-update) | async-done | bytes 4194320 | tf_op jit(solution)/shard_map/psum | solution.py:255
  1046.5 46.2 %reduce-scatter.15.cloned.1.call-done = bf16[32,256]{1,0:T(8,128)(2,1)} async-done(((bf16[512,256]{1,0:T(8,128)(2,1)}), bf16[32,256]{1,0:T(8,128)(2,1)}) %reduce-scatter.15.cloned.1.call-update) | async-done | bytes 16400 | tf_op jit(solution)/shard_map/reduce_scatter | solution.py:318
  1094.1 56.5 %reduce-scatter.17.cloned.1.call-done = bf16[32,256]{1,0:T(8,128)(2,1)} async-done(((bf16[512,256]{1,0:T(8,128)(2,1)}), bf16[32,256]{1,0:T(8,128)(2,1)}) %reduce-scatter.17.cloned.1.call-update) | async-done | bytes 16400 | tf_op jit(solution)/shard_map/reduce_scatter | solution.py:321
  1151.9 56.4 %reduce-scatter.13.cloned.1.call-done = bf16[32,256]{1,0:T(8,128)(2,1)} async-done(((bf16[512,256]{1,0:T(8,128)(2,1)}), bf16[32,256]{1,0:T(8,128)(2,1)}) %reduce-scatter.13.cloned.1.call-update) | async-done | bytes 16400 | tf_op jit(solution)/shard_map/reduce_scatter | solution.py:315
  1209.7 56.6 %reduce-scatter.19.cloned.1.call-done = bf16[256,32]{0,1:T(8,128)(2,1)} async-done(((bf16[256,512]{0,1:T(8,128)(2,1)}), bf16[256,32]{0,1:T(8,128)(2,1)}) %reduce-scatter.19.cloned.1.call-update) | async-done | bytes 16400 | tf_op jit(solution)/shard_map/reduce_scatter | solution.py:324
  1275.6 30.0 %all-reduce.13 = (bf16[512]{0:T(512)(128)(2,1)S(1)}, bf16[512]{0:T(512)(128)(2,1)S(1)}, bf16[512]{0:T(512)(128)(2,1)S(1)}, bf16[512]{0:T(512)(128)(2,1)S(1)}, bf...) all-reduce(bf16[512]{0:T(512)(128)(2,1)S(1)} %get-tuple-element.480, ...), channel_id=4, replica_groups=mesh['dp'=16,'tensor'=2] {'dp'}, use_global_device_ids=true, to_apply=%region_25.26.clone | all-reduce | flops 3584 | bytes 14336
  1308.0 16.0 %all-gather.11.cloned.1.call-done = bf16[4096,512]{1,0:T(8,128)(2,1)} async-done(((bf16[2048,512]{1,0:T(8,128)(2,1)}), bf16[4096,512]{1,0:T(8,128)(2,1)}) %all-gather.11.cloned.1.call-update) | async-done | bytes 4194320 | tf_op jit(solution)/shard_map/all_gather | solution.py:310
  (813 shorter events, 464.7 us)
Async XLA Ops:
  8.0 360.8 %all-reduce.17.cloned.1.call-start = ((), (), s32[]{:S(2)}) async-start(), calls=%async_computation.8 | async-start | bytes 8388608 | tf_op jit(solution)/shard_map/psum | solution.py:245
  10.9 35.2 %copy-start.27 = (f32[8,512]{1,0:T(8,128)}, f32[8,512]{1,0:T(8,128)S(1)}, u32[]{:S(2)}) copy-start(f32[8,512]{1,0:T(8,128)S(1)} %fusion.80) | copy-start | bytes 49156
  19.3 26.8 %copy-start.33 = (f32[512]{0:T(512)S(1)}, f32[512]{0:T(512)}, u32[]{:S(2)}) copy-start(f32[512]{0:T(512)} %param.49) | copy-start | bytes 6148
  19.3 26.8 %copy-start.44 = (f32[512]{0:T(512)S(1)}, f32[512]{0:T(512)}, u32[]{:S(2)}) copy-start(f32[512]{0:T(512)} %param.50) | copy-start | bytes 6148
  58.6 24.3 %copy-start.10 = (bf16[4096,512]{1,0:T(8,128)(2,1)S(1)}, bf16[4096,512]{1,0:T(8,128)(2,1)}, u32[]{:S(2)}) copy-start(bf16[4096,512]{1,0:T(8,128)(2,1)} %copy-done.9) | copy-start | bytes 12582916
  93.9 25.2 %copy-start.11 = (bf16[4096,512]{1,0:T(8,128)(2,1)S(1)}, bf16[4096,512]{1,0:T(8,128)(2,1)}, u32[]{:S(2)}) copy-start(bf16[4096,512]{1,0:T(8,128)(2,1)} %copy-done.9) | copy-start | bytes 12582916
  240.8 18.2 %copy-start.3 = (bf16[32,8,8,512]{3,1,2,0:T(8,128)(2,1)}, bf16[32,8,8,512]{3,1,2,0:T(8,128)(2,1)S(1)}, u32[]{:S(2)}) copy-start(bf16[32,8,8,512]{3,1,2,0:T(8,128)(2,1)S(1)} %copy.156) | copy-start | bytes 6291460
  262.3 106.5 %copy-start.28 = (f32[8,512]{1,0:T(8,128)S(1)}, f32[8,512]{1,0:T(8,128)}, u32[]{:S(2)}) copy-start(f32[8,512]{1,0:T(8,128)} %copy-done.27) | copy-start | bytes 49156
  262.3 114.8 %all-gather.5.cloned.1.call-start = ((), (), s32[]{:S(2)}) async-start(), calls=%async_computation.9 | async-start | bytes 1114112 | tf_op jit(solution)/shard_map/all_gather | solution.py:219
  262.9 129.9 %all-gather.7.cloned.1.call-start = ((), (), s32[]{:S(2)}) async-start(), calls=%async_computation.10 | async-start | bytes 1114112 | tf_op jit(solution)/shard_map/all_gather | solution.py:220
  263.5 214.9 %reduce-scatter.9.cloned.1.call-start = ((), (), s32[]{:S(2)}) async-start(), calls=%async_computation.12 | async-start | bytes 6291456 | tf_op jit(solution)/shard_map/reduce_scatter | solution.py:272
  392.8 24.6 %copy-start.46 = (bf16[512,1024]{1,0:T(8,128)(2,1)S(1)}, bf16[512,1024]{1,0:T(8,128)(2,1)}, u32[]{:S(2)}) copy-start(bf16[512,1024]{1,0:T(8,128)(2,1)} %all-gather.5.cloned.1.call-done) | copy-start | bytes 3145732
  423.9 121.0 %all-gather.9.cloned.1.call-start = ((), (), s32[]{:S(2)}) async-start(), calls=%async_computation.13 | async-start | bytes 6291456 | tf_op jit(solution)/shard_map/all_gather | solution.py:282
  488.0 314.5 %reduce-scatter.11.cloned.1.call-start = ((), (), s32[]{:S(2)}) async-start(), calls=%async_computation.14 | async-start | bytes 6291456 | tf_op jit(solution)/shard_map/reduce_scatter | solution.py:299
  748.1 115.8 %reduce-scatter.21.cloned.1.call-start = ((), (), s32[]{:S(2)}) async-start(), calls=%async_computation.20 | async-start | bytes 1114112 | tf_op jit(solution)/shard_map/reduce_scatter | solution.py:327
  760.6 163.2 %reduce-scatter.23.cloned.1.call-start = ((), (), s32[]{:S(2)}) async-start(), calls=%async_computation.21 | async-start | bytes 1114112 | tf_op jit(solution)/shard_map/reduce_scatter | solution.py:330
  771.1 262.8 %all-reduce.19.cloned.1.call-start = ((), (), s32[]{:S(2)}) async-start(), calls=%async_computation.11 | async-start | bytes 8388608 | tf_op jit(solution)/shard_map/psum | solution.py:255
  780.7 312.1 %reduce-scatter.15.cloned.1.call-start = ((), (), s32[]{:S(2)}) async-start(), calls=%async_computation.17 | async-start | bytes 278528 | tf_op jit(solution)/shard_map/reduce_scatter | solution.py:318
  786.5 364.1 %reduce-scatter.17.cloned.1.call-start = ((), (), s32[]{:S(2)}) async-start(), calls=%async_computation.18 | async-start | bytes 278528 | tf_op jit(solution)/shard_map/reduce_scatter | solution.py:321
  791.4 416.9 %reduce-scatter.13.cloned.1.call-start = ((), (), s32[]{:S(2)}) async-start(), calls=%async_computation.16 | async-start | bytes 278528 | tf_op jit(solution)/shard_map/reduce_scatter | solution.py:315
  796.5 469.8 %reduce-scatter.19.cloned.1.call-start = ((), (), s32[]{:S(2)}) async-start(), calls=%async_computation.19 | async-start | bytes 278528 | tf_op jit(solution)/shard_map/reduce_scatter | solution.py:324
  801.2 522.8 %all-gather.11.cloned.1.call-start = ((), (), s32[]{:S(2)}) async-start(), calls=%async_computation.15 | async-start | bytes 6291456 | tf_op jit(solution)/shard_map/all_gather | solution.py:310
  810.8 223.1 %copy-start.42 = (f32[512]{0:T(512)S(1)}, f32[512]{0:T(512)}, u32[]{:S(2)}) copy-start(f32[512]{0:T(512)} %param.60) | copy-start | bytes 6148
  1042.0 233.7 %copy-start.43 = (bf16[1024]{0:T(1024)(128)(2,1)S(1)}, bf16[1024]{0:T(1024)(128)(2,1)}, u32[]{:S(2)}) copy-start(bf16[1024]{0:T(1024)(128)(2,1)} %get-tuple-element.493) | copy-start | bytes 6148
  (84 other events, 338.0 us)
Sparse Core Ops, SparseCore 0:
  262.4 106.2 all-reduce.16
  424.1 54.3 reduce-scatter.8
  488.1 56.7 all-gather.8
  748.2 54.2 reduce-scatter.10
  806.4 57.4 reduce-scatter.20
  867.4 56.3 reduce-scatter.22
  926.9 106.9 all-reduce.18
  1037.4 55.2 reduce-scatter.14
  1096.3 54.2 reduce-scatter.16
  1154.0 54.3 reduce-scatter.12
  1211.9 54.3 reduce-scatter.18
  1268.2 55.7 all-gather.10
Sparse Core Ops, SparseCore 1:
  265.2 36.5 all-gather.4
  304.0 37.0 all-gather.6
where the time goes:
time: 1350 us; the launch traced here: 1340 us
  waiting for transfers between devices  656 us (49%)
  local copies, waits for them, and re-layouts  258 us (19%)
  matrix products  152 us (11%)
  other arithmetic  120 us (9%)
  blocking collectives  118 us (9%)
  between operations  18.1 us (1%)
  loops' own time  13.5 us (1%)
    psum x1, waiting for transfers between devices, body(): lax.psum(unit_part.astype(jnp.bfloat16), 'tensor').astype(jnp.float32)  109 us
    psum x1, waiting for transfers between devices, body(): lax.psum(head_part.astype(jnp.bfloat16), 'tensor').astype(jnp.float32)  105 us
    reduce_scatter x1, waiting for transfers between devices, body(): lax.psum_scatter(grad_outer_w.astype(jnp.bfloat16), 'dp', scatter_dimensi...  58.4 us
    reduce_scatter x1, waiting for transfers between devices, body(): lax.psum_scatter(grad_out_w.astype(jnp.bfloat16), 'dp', scatter_dimension...  56.6 us
    reduce_scatter x1, waiting for transfers between devices, body(): lax.psum_scatter(grad_value_w.astype(jnp.bfloat16), 'dp', scatter_dimensi...  56.5 us
    reduce_scatter x1, waiting for transfers between devices, body(): lax.psum_scatter(grad_query_w.astype(jnp.bfloat16), 'dp', scatter_dimensi...  56.4 us
    all_gather x1, waiting for transfers between devices, body(): lax.all_gather((upstream_share + grad_mid_norm).astype(jnp.bfloat16), 'te...  54.5 us
    reduce_scatter x1, waiting for transfers between devices, body(): lax.psum_scatter(jnp.dot(grad_inner, inner_back.T, preferred_element_type...  48.9 us
  transfers between devices with their start and end apart: 14, of which 12 were waited for; matrix products, arithmetic and copies ran while one was open for 9% of the time, Pallas kernels for 0%

commit v1 on v0

v1 whole, which is shorter than its diff:
```python
import functools

import jax
import jax.numpy as jnp
from jax import lax
from jax.experimental import pallas as pl
from jax.experimental.pallas import tpu as pltpu
from jax.sharding import PartitionSpec as P

D = 512
HEAD_DIM = 64
SPAN = 512
LEFT = 10
RIGHT = 2
FF = 2048
PAIR = 2 * HEAD_DIM
PAIRS = D // PAIR
GROUPS = 2
EG = D // GROUPS
FG = FF // GROUPS
TOP = 16
KEYS = TOP + SPAN + 16
EXTRA = 128
NEGATIVE = -1e30
epsilon = 1e-05
F32 = jnp.float32
BF16 = jnp.bfloat16
VMEM_LIMIT = 56 * 1024 * 1024
FORWARD_BLOCKS = tuple((96, 96 * b, 96 * b) for b in range(5)) + ((32, 480, 416),)


def dot(a, b):
    return lax.dot_general(a, b, (((1,), (0,)), ((), ())), preferred_element_type=F32)


def dot_nt(a, b):
    return lax.dot_general(a, b, (((1,), (1,)), ((), ())), preferred_element_type=F32)


def dot_tn(a, b):
    return lax.dot_general(a, b, (((0,), (0,)), ((), ())), preferred_element_type=F32)


def iota(shape, dim):
    return lax.broadcasted_iota(jnp.int32, shape, dim)


def row_mean(v):
    return jnp.sum(v, axis=-1, keepdims=True) * (1.0 / D)


def normalize(v):
    center = v - row_mean(v)
    scale = lax.rsqrt(row_mean(center * center) + epsilon)
    return center * scale, scale


def fold_rows(v):
    total = v[0:8]
    for r in range(8, v.shape[0], 8):
        total = total + v[r : r + 8]
    return total


def masked_rows(meta, span, frames_ref, row0, rows):
    places = iota((rows, 1), 0) + row0
    hide_t = (places >= meta[1, span]) & (places < meta[1, span] + meta[2, span])
    columns = iota((1, D), 1)
    hide_f = (columns >= meta[3, span]) & (columns < meta[3, span] + meta[4, span])
    keep = jnp.where(hide_t, 0.0, 1.0) * jnp.where(hide_f, 0.0, 1.0)
    return frames_ref[pl.ds(row0, rows), :].astype(F32) * keep, keep


def load_slots(places, slots_ref, w_ref, sems, start):
    count, rows = slots_ref.shape[0], slots_ref.shape[1]
    for j in range(count):
        copy = pltpu.make_async_copy(
            slots_ref.at[j],
            w_ref.at[places[0, j], pl.ds(pl.multiple_of(places[1, j], 16), rows), :],
            sems.at[j],
        )
        if start:
            copy.start()
        else:
            copy.wait()


def low_half():
    return iota((1, PAIR), 1) < HEAD_DIM


def attention_forward_kernel(
    meta, places, frames_ref, ctx_k_ref, ctx_v_ref, norm_ref, slots_ref,
    n1_ref, q_ref, k_ref, v_ref, att_ref, mid_ref,
    w_ref, sems, ke_ref, ko_ref, ve_ref, vo_ref, bias_ref, ones_ref,
):
    step = pl.program_id(0)
    span = meta[0, 0] + step

    @pl.when(step == 0)
    def _():
        load_slots(places, slots_ref, w_ref, sems, True)
        r, c = iota((96, 256), 0), iota((96, 256), 1) % 128
        bias_ref[...] = jnp.where((c >= r + 6) & (c <= r + 18), 0.0, NEGATIVE)
        r, c = iota((256, 128), 0), iota((256, 128), 1)
        ones_ref[...] = jnp.where((r < 128) == (c < 64), 1.0, 0.0).astype(BF16)

    for r0 in range(0, SPAN, 128):
        masked, _ = masked_rows(meta, span, frames_ref, r0, 128)
        xhat, _ = normalize(masked)
        n1_ref[r0 : r0 + 128, :] = (xhat * norm_ref[0:1, :] + norm_ref[1:2, :]).astype(BF16)

    @pl.when(step == 0)
    def _():
        load_slots(places, slots_ref, w_ref, sems, False)

    k_ref[0, 0:TOP, :] = ctx_k_ref[0]
    v_ref[0, 0:TOP, :] = ctx_v_ref[0]
    k_ref[0, TOP + SPAN :, :] = jnp.zeros((16, D), BF16)
    v_ref[0, TOP + SPAN :, :] = jnp.zeros((16, D), BF16)
    n1 = n1_ref[...]
    for g in range(GROUPS):
        cols = slice(g * EG, (g + 1) * EG)
        q_ref[:, cols] = (dot(n1, w_ref[g, :, 0:EG]) * HEAD_DIM**-0.5).astype(BF16)
        k_ref[0, TOP : TOP + SPAN, cols] = dot(n1, w_ref[g, :, EG : 2 * EG]).astype(BF16)
        v_ref[0, TOP : TOP + SPAN, cols] = dot(n1, w_ref[g, :, 2 * EG : 3 * EG]).astype(BF16)

    even = iota((1, D), 1) % PAIR < HEAD_DIM
    zero = jnp.zeros((), BF16)
    for r0, rows in ((0, 144), (144, 144), (288, 128), (416, 128)):
        kb, vb = k_ref[0, r0 : r0 + rows, :], v_ref[0, r0 : r0 + rows, :]
        ke_ref[r0 : r0 + rows, :] = jnp.where(even, kb, zero)
        ko_ref[r0 : r0 + rows, :] = jnp.where(even, zero, kb)
        ve_ref[r0 : r0 + rows, :] = jnp.where(even, vb, zero)
        vo_ref[r0 : r0 + rows, :] = jnp.where(even, zero, vb)

    first = TOP - meta[5, span]
    for j in range(PAIRS):
        lanes = slice(j * PAIR, (j + 1) * PAIR)
        for rows, q0, w0 in FORWARD_BLOCKS:
            window = slice(w0, w0 + 128)
            keys = jnp.concatenate([ke_ref[window, lanes], ko_ref[window, lanes]], axis=0)
            scores = dot_nt(q_ref[q0 : q0 + rows, lanes], keys)
            if q0 == 480:
                r, c = iota((rows, 256), 0), iota((rows, 256), 1) % 128 - 64
                bias = jnp.where((c >= r + 6) & (c <= r + 18) & (c < 48), 0.0, NEGATIVE)
            else:
                bias = bias_ref[...]
            scores = scores + bias
            if q0 == 0:
                scores = jnp.where(iota((rows, 256), 1) % 128 >= first, scores, NEGATIVE)
            expo = []
            for half in (scores[:, :128], scores[:, 128:]):
                top = jnp.max(half, axis=-1, keepdims=True)
                expo.append(jnp.exp(half - top).astype(BF16))
            values = jnp.concatenate([ve_ref[window, lanes], vo_ref[window, lanes]], axis=0)
            values = jnp.concatenate([values, ones_ref[...]], axis=1)
            mixed = dot(jnp.concatenate(expo, axis=1), values)
            att_ref[q0 : q0 + rows, lanes] = (mixed[:, :PAIR] / mixed[:, PAIR:]).astype(BF16)

    att = att_ref[...]
    mid_ref[...] = dot_nt(att[:, :EG], w_ref[0, :, 3 * EG :]) + dot_nt(
        att[:, EG:], w_ref[1, :, 3 * EG :]
    )
    for r0 in range(0, SPAN, 128):
        masked, _ = masked_rows(meta, span, frames_ref, r0, 128)
        mid_ref[r0 : r0 + 128, :] = mid_ref[r0 : r0 + 128, :] + masked


def spec(block, index, **kw):
    return pl.BlockSpec(block, index, **kw)


def params():
    return pltpu.CompilerParams(
        dimension_semantics=("arbitrary",), vmem_limit_bytes=VMEM_LIMIT
    )


def attention_forward(meta, places, frames, ctx_k, ctx_v, norm, slots, spans):
    rows = spans * SPAN
    whole = pl.BlockSpec(memory_space=pl.ANY)
    row_block = spec((SPAN, D), lambda s, m, p: (s, 0))
    keys_block = spec((1, KEYS, D), lambda s, m, p: (s, 0, 0))
    flops = 2 * rows * D * D * 4 + 2 * rows * D * 640
    return pl.pallas_call(
        attention_forward_kernel,
        grid_spec=pltpu.PrefetchScalarGridSpec(
            num_scalar_prefetch=2,
            grid=(spans,),
            in_specs=[
                spec((SPAN, D), lambda s, m, p: (m[0, 0] + s, 0)),
                spec((1, TOP, D), lambda s, m, p: (m[0, 1] + s, 0, 0)),
                spec((1, TOP, D), lambda s, m, p: (m[0, 1] + s, 0, 0)),
                spec((8, D), lambda s, m, p: (0, 0)),
                whole,
            ],
            out_specs=[row_block, row_block, keys_block, keys_block, row_block, row_block],
            scratch_shapes=[
                pltpu.VMEM((GROUPS, D, 4 * EG), BF16),
                pltpu.SemaphoreType.DMA((slots.shape[0],)),
                pltpu.VMEM((KEYS, D), BF16),
                pltpu.VMEM((KEYS, D), BF16),
                pltpu.VMEM((KEYS, D), BF16),
                pltpu.VMEM((KEYS, D), BF16),
                pltpu.VMEM((96, 256), F32),
                pltpu.VMEM((256, 128), BF16),
            ],
        ),
        out_shape=[
            jax.ShapeDtypeStruct((rows, D), BF16),
            jax.ShapeDtypeStruct((rows, D), BF16),
            jax.ShapeDtypeStruct((spans, KEYS, D), BF16),
            jax.ShapeDtypeStruct((spans, KEYS, D), BF16),
            jax.ShapeDtypeStruct((rows, D), BF16),
            jax.ShapeDtypeStruct((rows, D), F32),
        ],
        compiler_params=params(),
        cost_estimate=pl.CostEstimate(
            flops=flops, bytes_accessed=rows * D * 14, transcendentals=rows * 1024
        ),
        name="attention_forward",
    )(meta, places, frames, ctx_k, ctx_v, norm, slots)


def feed_forward_kernel(
    meta, places, mid_ref, cot_ref, norm_ref, inner_b_ref, slots_ref,
    out_ref, gm_ref, grad_ref, sums_ref, sums_b_ref,
    w_ref, sems, n2_ref, n2t_ref, cott_ref, hid_ref, gin_ref, dn_ref, acc_ref,
):
    step = pl.program_id(0)

    @pl.when(step == 0)
    def _():
        load_slots(places, slots_ref, w_ref, sems, True)
        acc_ref[...] = jnp.zeros_like(acc_ref)
        sums_ref[...] = jnp.zeros_like(sums_ref)
        sums_b_ref[...] = jnp.zeros_like(sums_b_ref)

    for r0 in range(0, SPAN, 128):
        xhat, _ = normalize(mid_ref[r0 : r0 + 128, :])
        n2_ref[r0 : r0 + 128, :] = (xhat * norm_ref[2:3, :] + norm_ref[3:4, :]).astype(BF16)
    n2t_ref[...] = n2_ref[...].T
    cott_ref[...] = cot_ref[...].T

    @pl.when(step == 0)
    def _():
        load_slots(places, slots_ref, w_ref, sems, False)

    chunk = 256
    for g in range(GROUPS):
        for c0 in range(0, FG, chunk):
            cols = slice(g * FG + c0, g * FG + c0 + chunk)
            act = dot(n2_ref[...], w_ref[g, :, c0 : c0 + chunk]) + inner_b_ref[0:1, cols]
            square = act * act
            tanh = jnp.tanh(act * (0.7978845608 + (0.7978845608 * 0.044715) * square))
            weight = 0.5 + 0.5 * tanh
            hidden = act * weight
            hid_ref[:, cols] = hidden.astype(BF16)
            slope = weight + (hidden - hidden * weight) * (
                2.0 * 0.7978845608 + (6.0 * 0.7978845608 * 0.044715) * square
            )
            grad = dot(cot_ref[...], w_ref[g, :, FG + c0 : FG + c0 + chunk]) * slope
            grad_low = grad.astype(BF16)
            gin_ref[:, cols] = grad_low
            sums_b_ref[:, cols] += fold_rows(grad_low.astype(F32))

    hid, gin = hid_ref, gin_ref
    out_ref[...] = (
        mid_ref[...]
        + dot_nt(hid[:, :FG], w_ref[0, :, FG:])
        + dot_nt(hid[:, FG:], w_ref[1, :, FG:])
        + norm_ref[4:5, :]
    ).astype(BF16)
    dn_ref[...] = dot_nt(gin[:, :FG], w_ref[0, :, :FG]) + dot_nt(gin[:, FG:], w_ref[1, :, :FG])
    for g in range(GROUPS):
        cols = slice(g * FG, (g + 1) * FG)
        acc_ref[g, :, :FG] += dot(n2t_ref[...], gin[:, cols])
        acc_ref[g, :, FG:] += dot(cott_ref[...], hid[:, cols])

    for r0 in range(0, SPAN, 128):
        rows = slice(r0, r0 + 128)
        xhat, scale = normalize(mid_ref[rows, :])
        grad = dn_ref[rows, :]
        cot = cot_ref[rows, :].astype(F32)
        sums_ref[0:8, :] += fold_rows(grad * xhat)
        sums_ref[8:16, :] += fold_rows(grad)
        sums_ref[16:24, :] += fold_rows(cot)
        t = grad * norm_ref[2:3, :]
        gm_ref[rows, :] = (cot + scale * (t - row_mean(t) - xhat * row_mean(t * xhat))).astype(BF16)

    @pl.when(step == pl.num_programs(0) - 1)
    def _():
        for g in range(GROUPS):
            grad_ref[g, :, : 2 * FG] = acc_ref[g].astype(BF16)
        grad_ref[:, :, 2 * FG :] = jnp.zeros((GROUPS, D, EXTRA), BF16)


def feed_forward(meta, places, mid, cot, norm, inner_b, slots, spans):
    rows = spans * SPAN
    whole = pl.BlockSpec(memory_space=pl.ANY)
    row_block = spec((SPAN, D), lambda s, m, p: (s, 0))
    return pl.pallas_call(
        feed_forward_kernel,
        grid_spec=pltpu.PrefetchScalarGridSpec(
            num_scalar_prefetch=2,
            grid=(spans,),
            in_specs=[
                row_block,
                spec((SPAN, D), lambda s, m, p: (m[0, 0] + s, 0)),
                spec((8, D), lambda s, m, p: (0, 0)),
                spec((1, FF), lambda s, m, p: (0, 0)),
                whole,
            ],
            out_specs=[
                row_block,
                row_block,
                spec((GROUPS, D, 2 * FG + EXTRA), lambda s, m, p: (0, 0, 0)),
                spec((24, D), lambda s, m, p: (0, 0)),
                spec((8, FF), lambda s, m, p: (0, 0)),
            ],
            scratch_shapes=[
                pltpu.VMEM((GROUPS, D, 2 * FG), BF16),
                pltpu.SemaphoreType.DMA((slots.shape[0],)),
                pltpu.VMEM((SPAN, D), BF16),
                pltpu.VMEM((D, SPAN), BF16),
                pltpu.VMEM((D, SPAN), BF16),
                pltpu.VMEM((SPAN, FF), BF16),
                pltpu.VMEM((SPAN, FF), BF16),
                pltpu.VMEM((SPAN, D), F32),
                pltpu.VMEM((GROUPS, D, 2 * FG), F32),
            ],
        ),
        out_shape=[
            jax.ShapeDtypeStruct((rows, D), BF16),
            jax.ShapeDtypeStruct((rows, D), BF16),
            jax.ShapeDtypeStruct((GROUPS, D, 2 * FG + EXTRA), BF16),
            jax.ShapeDtypeStruct((24, D), F32),
            jax.ShapeDtypeStruct((8, FF), F32),
        ],
        compiler_params=params(),
        cost_estimate=pl.CostEstimate(
            flops=12 * rows * D * FF, bytes_accessed=rows * D * 10, transcendentals=rows * FF
        ),
        name="feed_forward",
    )(meta, places, mid, cot, norm, inner_b, slots)


def attention_backward_kernel(
    meta, places, frames_ref, n1_ref, q_ref, k_ref, v_ref, att_ref, gm_ref, norm_ref, slots_ref,
    gf_ref, gck_ref, gcv_ref, grad_ref, sums_ref,
    w_ref, sems, gatt_ref, dq_ref, dk_ref, dv_ref, dkb_ref, dvb_ref, n1t_ref, gmt_ref, dn_ref,
    bias_ref, acc_ref,
):
    step = pl.program_id(0)
    span = meta[0, 0] + step

    @pl.when(step == 0)
    def _():
        load_slots(places, slots_ref, w_ref, sems, True)
        acc_ref[...] = jnp.zeros_like(acc_ref)
        sums_ref[...] = jnp.zeros_like(sums_ref)
        r, c = iota((160, 256), 0), iota((160, 256), 1) % 128
        bias_ref[...] = jnp.where((r >= c + 6) & (r <= c + 18), 0.0, NEGATIVE)

    n1t_ref[...] = n1_ref[...].T
    gmt_ref[...] = gm_ref[...].T

    @pl.when(step == 0)
    def _():
        load_slots(places, slots_ref, w_ref, sems, False)

    for g in range(GROUPS):
        gatt_ref[:, g * EG : (g + 1) * EG] = dot(gm_ref[...], w_ref[g, :, 3 * EG :]).astype(BF16)

    first = TOP - meta[5, span]
    even = low_half()
    zero = jnp.zeros((), BF16)
    for j in range(PAIRS):
        lanes = slice(j * PAIR, (j + 1) * PAIR)
        for b in range(SPAN // 128):
            rows, window = slice(128 * b, 128 * b + 128), slice(128 * b, 128 * b + 160)
            kw, vw = k_ref[0, window, lanes], v_ref[0, window, lanes]
            qb, ob = q_ref[rows, lanes], gatt_ref[rows, lanes]
            qs = jnp.concatenate([jnp.where(even, qb, zero), jnp.where(even, zero, qb)], axis=0)
            os = jnp.concatenate([jnp.where(even, ob, zero), jnp.where(even, zero, ob)], axis=0)
            scores = dot_nt(kw, qs) + bias_ref[...]
            if b == 0:
                scores = jnp.where(iota((160, 256), 0) >= first, scores, NEGATIVE)
            if b == SPAN // 128 - 1:
                scores = jnp.where(iota((160, 256), 0) < 144, scores, NEGATIVE)
            expo = jnp.exp(scores - jnp.max(scores, axis=0, keepdims=True))
            probs = expo * (1.0 / jnp.sum(expo, axis=0, keepdims=True))
            grad_probs = dot_nt(vw, os)
            delta = jnp.sum(probs * grad_probs, axis=0, keepdims=True)
            ds = (probs * (grad_probs - delta)).astype(BF16)
            dv = dot(probs.astype(BF16), os)
            dk = dot(ds, qs)
            if b == 0:
                dkb_ref[window, lanes] = dk
                dvb_ref[window, lanes] = dv
            else:
                lap, rest = slice(128 * b, 128 * b + 32), slice(128 * b + 32, 128 * b + 160)
                dkb_ref[lap, lanes] += dk[:32]
                dvb_ref[lap, lanes] += dv[:32]
                dkb_ref[rest, lanes] = dk[32:]
                dvb_ref[rest, lanes] = dv[32:]
            dq = dot_tn(ds, kw)
            dq = jnp.where(even, dq[:128], dq[128:]) * HEAD_DIM**-0.5
            dq_ref[rows, lanes] = dq.astype(BF16)
    gck_ref[0] = dkb_ref[0:TOP, :]
    gcv_ref[0] = dvb_ref[0:TOP, :]
    dk_ref[...] = dkb_ref[TOP : TOP + SPAN, :].astype(BF16)
    dv_ref[...] = dvb_ref[TOP : TOP + SPAN, :].astype(BF16)

    for g in range(GROUPS):
        cols = slice(g * EG, (g + 1) * EG)
        acc_ref[g, :, 0:EG] += dot(n1t_ref[...], dq_ref[:, cols])
        acc_ref[g, :, EG : 2 * EG] += dot(n1t_ref[...], dk_ref[:, cols])
        acc_ref[g, :, 2 * EG : 3 * EG] += dot(n1t_ref[...], dv_ref[:, cols])
        acc_ref[g, :, 3 * EG :] += dot(gmt_ref[...], att_ref[:, cols])
    total = None
    for g in range(GROUPS):
        cols = slice(g * EG, (g + 1) * EG)
        for m, ref in enumerate((dq_ref, dk_ref, dv_ref)):
            term = dot_nt(ref[:, cols], w_ref[g, :, m * EG : (m + 1) * EG])
            total = term if total is None else total + term
    dn_ref[...] = total
    for r0 in range(0, SPAN, 128):
        rows = slice(r0, r0 + 128)
        masked, keep = masked_rows(meta, span, frames_ref, r0, 128)
        xhat, scale = normalize(masked)
        grad = dn_ref[rows, :]
        sums_ref[0:8, :] += fold_rows(grad * xhat)
        sums_ref[8:16, :] += fold_rows(grad)
        t = grad * norm_ref[0:1, :]
        back = scale * (t - row_mean(t) - xhat * row_mean(t * xhat))
        gf_ref[rows, :] = ((gm_ref[rows, :].astype(F32) + back) * keep).astype(BF16)

    @pl.when(step == pl.num_programs(0) - 1)
    def _():
        for g in range(GROUPS):
            grad_ref[g, :, : 4 * EG] = acc_ref[g].astype(BF16)
        grad_ref[:, :, 4 * EG :] = jnp.zeros((GROUPS, D, EXTRA), BF16)


def attention_backward(meta, places, frames, n1, q, k, v, att, gm, norm, slots, spans):
    rows = spans * SPAN
    whole = pl.BlockSpec(memory_space=pl.ANY)
    row_block = spec((SPAN, D), lambda s, m, p: (s, 0))
    keys_block = spec((1, KEYS, D), lambda s, m, p: (s, 0, 0))
    top_block = spec((1, TOP, D), lambda s, m, p: (s, 0, 0))
    low = pltpu.VMEM((SPAN, D), BF16)
    return pl.pallas_call(
        attention_backward_kernel,
        grid_spec=pltpu.PrefetchScalarGridSpec(
            num_scalar_prefetch=2,
            grid=(spans,),
            in_specs=[
                spec((SPAN, D), lambda s, m, p: (m[0, 0] + s, 0)),
                row_block,
                row_block,
                keys_block,
                keys_block,
                row_block,
                row_block,
                spec((8, D), lambda s, m, p: (0, 0)),
                whole,
            ],
            out_specs=[
                row_block,
                top_block,
                top_block,
                spec((GROUPS, D, 4 * EG + EXTRA), lambda s, m, p: (0, 0, 0)),
                spec((16, D), lambda s, m, p: (0, 0)),
            ],
            scratch_shapes=[
                pltpu.VMEM((GROUPS, D, 4 * EG), BF16),
                pltpu.SemaphoreType.DMA((slots.shape[0],)),
                low,
                low,
                low,
                low,
                pltpu.VMEM((KEYS, D), F32),
                pltpu.VMEM((KEYS, D), F32),
                low,
                low,
                pltpu.VMEM((SPAN, D), F32),
                pltpu.VMEM((160, 256), F32),
                pltpu.VMEM((GROUPS, D, 4 * EG), F32),
            ],
        ),
        out_shape=[
            jax.ShapeDtypeStruct((rows, D), BF16),
            jax.ShapeDtypeStruct((spans, TOP, D), F32),
            jax.ShapeDtypeStruct((spans, TOP, D), F32),
            jax.ShapeDtypeStruct((GROUPS, D, 4 * EG + EXTRA), BF16),
            jax.ShapeDtypeStruct((16, D), F32),
        ],
        compiler_params=params(),
        cost_estimate=pl.CostEstimate(
            flops=2 * rows * D * D * 8 + 2 * rows * D * 1600,
            bytes_accessed=rows * D * 14,
            transcendentals=rows * 1280,
        ),
        name="attention_backward",
    )(meta, places, frames, n1, q, k, v, att, gm, norm, slots)


BITS = {"core": ("dp", 1), "y": ("dp", 2), "z1": ("dp", 4), "z2": ("dp", 8), "x": ("tensor", 1)}
BIT_DIM = {"z2": 1, "z1": 2, "y": 3, "core": 4, "x": 0}


def swap(value, bit):
    axis, distance = BITS[bit]
    count = lax.axis_size(axis)
    return lax.ppermute(value, axis, [(i, i ^ distance) for i in range(count)])


def my_bit(bit):
    axis, distance = BITS[bit]
    return (lax.axis_index(axis) // distance) % 2


def gather_slots(piece, order):
    held = piece[None]
    for bit in order:
        held = jnp.concatenate([held, swap(held, bit)], axis=0)
    return held


def slot_places(order, rows):
    groups, firsts = [], []
    dp, tensor = lax.axis_index("dp"), lax.axis_index("tensor")
    for j in range(2 ** len(order)):
        dp_flip = sum(BITS[b][1] for i, b in enumerate(order) if j >> i & 1 and b != "x")
        x_flip = sum(1 for i, b in enumerate(order) if j >> i & 1 and b == "x")
        groups.append(tensor ^ x_flip)
        firsts.append((dp ^ dp_flip) * rows)
    return jnp.stack([jnp.stack(groups), jnp.stack(firsts)]).astype(jnp.int32)


def scatter_sum(grad, order):
    columns = grad.shape[-1]
    held = grad.reshape(2, 2, 2, 2, 2, -1, columns)
    for bit in order:
        dim, mine = BIT_DIM[bit], my_bit(bit)
        keep = lax.dynamic_index_in_dim(held, mine, dim, keepdims=True)
        send = lax.dynamic_index_in_dim(held, 1 - mine, dim, keepdims=True)
        held = (keep.astype(F32) + swap(send, bit).astype(F32)).astype(BF16)
    return held.reshape(-1, columns)


ATTENTION_ORDER = ("z2", "z1", "y", "x", "core")
FEED_ORDER = ("z2", "z1", "x", "y", "core")
ATTENTION_SUM = ("core", "x", "y", "z1", "z2")
FEED_SUM = ("core", "y", "z1", "z2", "x")


def body(
    frames,
    context_keys,
    context_values,
    time_start,
    time_width,
    freq_start,
    freq_width,
    context_count,
    gain_one,
    shift_one,
    query_w,
    key_w,
    value_w,
    out_w,
    gain_two,
    shift_two,
    inner_w,
    inner_b,
    outer_w,
    outer_b,
    cotangent,
):
    tensor, dp = lax.axis_size("tensor"), lax.axis_size("dp")
    tuned = tensor == 2 and dp == 16
    spans = time_start.shape[0] // tensor
    t_index = lax.axis_index("tensor")
    base = t_index * spans

    attention_piece = jnp.concatenate([query_w, key_w, value_w, out_w.T], axis=1)
    feed_piece = jnp.concatenate([inner_w, outer_w.T], axis=1)
    inner_b_full = lax.all_gather(inner_b, "tensor", axis=0, tiled=True).reshape(1, FF)
    if tuned:
        attention_slots = gather_slots(attention_piece, ATTENTION_ORDER)
        feed_slots = gather_slots(feed_piece, FEED_ORDER)
        attention_places = slot_places(ATTENTION_ORDER, attention_piece.shape[0])
        feed_places = slot_places(FEED_ORDER, feed_piece.shape[0])
    else:
        def canonical(parts, width):
            grouped = []
            for part in parts:
                whole = lax.all_gather(part, "dp", axis=0, tiled=True)
                whole = lax.all_gather(whole, "tensor", axis=1, tiled=True)
                grouped.append(whole.reshape(D, GROUPS, width).swapaxes(0, 1))
            return jnp.concatenate(grouped, axis=2)

        attention_slots = canonical((query_w, key_w, value_w, out_w.T), EG)
        feed_slots = canonical((inner_w, outer_w.T), FG)
        attention_places = feed_places = jnp.array([[0, 1], [0, 0]], jnp.int32)

    context = jnp.stack([context_keys, context_values])
    context = lax.all_to_all(context, "tensor", split_axis=1, concat_axis=3, tiled=True)
    context = jnp.pad(context, ((0, 0), (0, 0), (TOP - LEFT, 0), (0, 0)))

    first_row = jnp.zeros_like(time_start).at[0].set(base)
    meta = jnp.stack(
        [first_row, time_start, time_width, freq_start, freq_width, context_count]
    ).astype(jnp.int32)
    norm = jnp.stack(
        [gain_one, shift_one, gain_two, shift_two, outer_b]
        + [jnp.zeros_like(gain_one)] * 3
    )

    n1, q, k, v, att, mid = attention_forward(
        meta, attention_places, frames, context[0], context[1], norm, attention_slots, spans
    )
    out_half, gm, feed_grad, sums_two, sums_b = feed_forward(
        meta, feed_places, mid, cotangent, norm, inner_b_full, feed_slots, spans
    )
    frames_half, gck, gcv, attention_grad, sums_one = attention_backward(
        meta, attention_places, frames, n1, q, k, v, att, gm, norm, attention_slots, spans
    )

    def both(half):
        if not tuned:
            return lax.all_gather(half, "tensor", axis=0, tiled=True)
        other = swap(half, "x")
        rows = half.shape[0]
        whole = jnp.zeros((2 * rows, D), half.dtype)
        whole = lax.dynamic_update_slice_in_dim(whole, half, t_index * rows, 0)
        return lax.dynamic_update_slice_in_dim(whole, other, (1 - t_index) * rows, 0)

    output = both(out_half)
    grad_frames = both(frames_half)
    grad_context = jnp.stack([gck, gcv])[:, :, TOP - LEFT :]
    grad_context = lax.all_to_all(grad_context, "tensor", split_axis=3, concat_axis=1, tiled=True)

    gain_two_sum, shift_two_sum, outer_b_sum = (
        jnp.sum(sums_two[8 * i : 8 * i + 8], axis=0) for i in range(3)
    )
    gain_one_sum, shift_one_sum = (jnp.sum(sums_one[8 * i : 8 * i + 8], axis=0) for i in range(2))
    inner_b_sum = jnp.sum(sums_b, axis=0)

    if tuned:
        def shared(item):
            return jnp.broadcast_to(item.reshape(1, dp, -1), (GROUPS, dp, D // dp))

        def with_extra(grad, vectors):
            row = jnp.concatenate(vectors, axis=2).astype(BF16)
            row = jnp.pad(row, ((0, 0), (0, 0), (0, 2 * EXTRA - row.shape[2])))
            block = row.reshape(GROUPS, dp, 2, EXTRA)
            block = jnp.pad(block, ((0, 0), (0, 0), (0, D // dp - 2), (0, 0)))
            block = block.reshape(GROUPS, D, EXTRA)
            return lax.dynamic_update_slice(grad, block, (0, 0, grad.shape[2] - EXTRA))

        feed_sum = scatter_sum(
            with_extra(
                feed_grad,
                [inner_b_sum.reshape(GROUPS, dp, -1)]
                + [shared(item) for item in (gain_two_sum, shift_two_sum, outer_b_sum)],
            ),
            FEED_SUM,
        ).astype(F32)
        attention_sum = scatter_sum(
            with_extra(attention_grad, [shared(gain_one_sum), shared(shift_one_sum)]), ATTENTION_SUM
        ).astype(F32)
        extra = feed_sum[:2, 2 * FG :].reshape(-1)
        sum_inner_b, sum_gain_two, sum_shift_two, sum_outer_b = (
            extra[:64], extra[64:96], extra[96:128], extra[128:160]
        )
        extra = attention_sum[0, 4 * EG :]
        sum_gain_one, sum_shift_one = extra[:32], extra[32:64]
        sum_query, sum_key, sum_value, sum_out = (
            attention_sum[:, i * EG : (i + 1) * EG] for i in range(4)
        )
        sum_inner, sum_outer = feed_sum[:, :FG], feed_sum[:, FG : 2 * FG]
    else:
        def whole_grad(grad, index, width):
            return grad[:, :, index * width : (index + 1) * width].swapaxes(0, 1).reshape(D, -1)

        def scattered(grad):
            part = lax.psum_scatter(grad, "dp", scatter_dimension=0, tiled=True)
            return lax.psum_scatter(part, "tensor", scatter_dimension=1, tiled=True).astype(F32)

        def vector(item):
            item = lax.psum(item, "tensor")
            return lax.psum_scatter(item, "dp", scatter_dimension=0, tiled=True)

        sum_query, sum_key, sum_value, sum_out = (
            scattered(whole_grad(attention_grad, i, EG)) for i in range(4)
        )
        sum_inner, sum_outer = (scattered(whole_grad(feed_grad, i, FG)) for i in range(2))
        sum_gain_one, sum_shift_one = vector(gain_one_sum), vector(shift_one_sum)
        sum_gain_two, sum_shift_two = vector(gain_two_sum), vector(shift_two_sum)
        sum_outer_b = vector(outer_b_sum)
        sum_inner_b = lax.psum_scatter(inner_b_sum, "tensor", scatter_dimension=0, tiled=True)
        sum_inner_b = lax.psum_scatter(sum_inner_b, "dp", scatter_dimension=0, tiled=True)

    return (
        output,
        grad_frames,
        grad_context[0],
        grad_context[1],
        sum_gain_one,
        sum_shift_one,
        sum_query,
        sum_key,
        sum_value,
        sum_out.T,
        sum_gain_two,
        sum_shift_two,
        sum_inner,
        sum_inner_b,
        sum_outer.T,
        sum_outer_b,
    )


def solution(mesh):
    in_specs = (
        P("dp", None),
        P("dp", None, "tensor"),
        P("dp", None, "tensor"),
        P("dp"),
        P("dp"),
        P("dp"),
        P("dp"),
        P("dp"),
        P(),
        P(),
        P("dp", "tensor"),
        P("dp", "tensor"),
        P("dp", "tensor"),
        P("tensor", "dp"),
        P(),
        P(),
        P("dp", "tensor"),
        P("tensor"),
        P("tensor", "dp"),
        P(),
        P("dp", None),
    )
    out_specs = (
        P("dp", None),
        P("dp", None),
        P("dp", None, "tensor"),
        P("dp", None, "tensor"),
        P("dp"),
        P("dp"),
        P("dp", "tensor"),
        P("dp", "tensor"),
        P("dp", "tensor"),
        P("tensor", "dp"),
        P("dp"),
        P("dp"),
        P("dp", "tensor"),
        P(("tensor", "dp")),
        P("tensor", "dp"),
        P("dp"),
    )
    return jax.shard_map(body, mesh=mesh, in_specs=in_specs, out_specs=out_specs, check_vma=False)
```

time: 1350 us -> 386 us (0.29)
  waiting for transfers between devices: 656 us -> 174 us
  local copies, waits for them, and re-layouts: 258 us -> 47.5 us
  matrix products: 152 us -> 0 us
  blocking collectives: 118 us -> 4.43 us
  other arithmetic: 120 us -> 14.2 us
  Pallas kernels: 0 us -> 99.9 us
  starting transfers between devices: 1.41 us -> 43.6 us
  between operations: 18.1 us -> 1.47 us
  loops' own time: 13.5 us -> 0 us
    reduce_scatter x8 -> x0, waiting for transfers between devices: 370 us -> none  [the longest x1 58.4 us: body(): lax.psum_scatter(grad_outer_w.astype(jnp.bfloat16), 'dp', scatter_dimensi...]
    psum x2 -> x0, waiting for transfers between devices: 214 us -> none  [the longest x1 109 us: body(): lax.psum(unit_part.astype(jnp.bfloat16), 'tensor').astype(jnp.float32)]
    ppermute x0 -> x22, waiting for transfers between devices: none -> 174 us  [swap(): return lax.ppermute(value, axis, [(i, i ^ distance) for i in range(count)])]
    dot_general x74 -> x0, matrix products: 152 us -> none  [the longest x1 21.4 us: body(): jnp.dot(cotangent, outer_back.T, preferred_element_type=jnp.float32)]
    pallas_call x0 -> x3, Pallas kernels: none -> 99.9 us  [the longest x1 43.1 us: feed_forward(): pl.pallas_call(feed_forward_kernel, grid_spec=pltpu.PrefetchScalarGridSpe...]
    all_gather x4 -> x1, blocking collectives: 80 us -> 4.43 us  [body(): lax.all_gather(inner_b, 'tensor', axis=0, tiled=True).reshape(1, FF)]
    all_gather x4 -> x0, waiting for transfers between devices: 70.6 us -> none  [the longest x1 54.5 us: body(): lax.all_gather((upstream_share + grad_mid_norm).astype(jnp.bfloat16), 'te...]
    slice x38 -> x7, local copies, waits for them, and re-layouts: 50.8 us -> 2.84 us  [the longest x1 1.1 us: body(): grad_context = jnp.stack([gck, gcv])[:, :, TOP - LEFT:]]
  transfers between devices with their start and end apart: 14 -> 24, of which waited for: 12 -> 12; matrix products, arithmetic and copies ran while one was open for 9% -> 13% of each run, Pallas kernels for 0% -> 5%
where the time goes in v1:
time: 386 us; the launch traced here: 385 us
  waiting for transfers between devices  174 us (45%)
  Pallas kernels  99.9 us (26%)
  local copies, waits for them, and re-layouts  47.5 us (12%)
  starting transfers between devices  43.6 us (11%)
  other arithmetic  14.2 us (4%)
  blocking collectives  4.43 us (1%)
    ppermute x22, waiting for transfers between devices, swap(): return lax.ppermute(value, axis, [(i, i ^ distance) for i in range(count)])  174 us
    pallas_call x1, Pallas kernels, feed_forward(): pl.pallas_call(feed_forward_kernel, grid_spec=pltpu.PrefetchScalarGridSpe...  43.1 us
    pallas_call x1, Pallas kernels, attention_backward(): pl.pallas_call(attention_backward_kernel, grid_spec=pltpu.PrefetchScalarG...  39.2 us
    ppermute x22, starting transfers between devices, swap(): return lax.ppermute(value, axis, [(i, i ^ distance) for i in range(count)])  36.6 us
    pallas_call x1, Pallas kernels, attention_forward(): pl.pallas_call(attention_forward_kernel, grid_spec=pltpu.PrefetchScalarGr...  17.6 us
    unnamed x68, local copies, waits for them, and re-layouts  15.4 us
  transfers between devices with their start and end apart: 24, of which 12 were waited for; matrix products, arithmetic and copies ran while one was open for 13% of the time, Pallas kernels for 5%

profile of v1, /device:TPU:0, one launch (start us, length us, event | category | flops | bytes accessed | tf_op | source)
XLA Modules:
  0.0 385.2 jit_solution(17545482214390366629)
XLA Ops:
  1.6 4.1 %collective-permute-start.5 = (bf16[1,32,2048]{2,1,0:T(8,128)(2,1)S(1)}, bf16[1,32,2048]{2,1,0:T(8,128)(2,1)S(1)}, u32[]{:S(2)}, u32[]{:S(2)}) collective-permute-start(bf16[1,32,2048]{2,1,0:T(8,128)(2,1)S(1)} %maximum_bitcast_fusion), channel_id=1, source_target_pairs={{0,16},{2,18},{4,20},{6,22},{8,24},{10,26},{12,28},{14,30},{16,0},... | collective-permute-start | bytes 393224 | tf_op jit(solution)/shard_map/ppermute | solution.py:517
  5.7 6.3 %collective-permute-done.5 = bf16[1,32,2048]{2,1,0:T(8,128)(2,1)S(1)} collective-permute-done((bf16[1,32,2048]{2,1,0:T(8,128)(2,1)S(1)}, bf16[1,32,2048]{2,1,0:T(8,128)(2,1)S(1)}, u32[]{:S(2)}, u32[]{:S(2)}) %collective-permute-start.5) | collective-permute-done | bytes 131104 | tf_op jit(solution)/shard_map/ppermute | solution.py:517
  12.8 6.8 %collective-permute-done.6 = bf16[2,32,2048]{2,1,0:T(8,128)(2,1)S(1)} collective-permute-done((bf16[2,32,2048]{2,1,0:T(8,128)(2,1)S(1)}, bf16[2,32,2048]{2,1,0:T(8,128)(2,1)S(1)}, u32[]{:S(2)}, u32[]{:S(2)}) %collective-permute-start.6) | collective-permute-done | bytes 262176 | tf_op jit(solution)/shard_map/ppermute | solution.py:517
  21.7 3.4 collective-permute-start
  36.2 24.0 %collective-permute-done.2 = bf16[4,32,1024]{2,1,0:T(8,128)(2,1)S(1)} collective-permute-done((bf16[4,32,1024]{2,1,0:T(8,128)(2,1)S(1)}, bf16[4,32,1024]{2,1,0:T(8,128)(2,1)S(1)}, u32[]{:S(2)}, u32[]{:S(2)}) %collective-permute-start.2) | collective-permute-done | bytes 262176 | tf_op jit(solution)/shard_map/ppermute | solution.py:517
  65.8 4.9 %collective-permute-done.3 = bf16[8,32,1024]{2,1,0:T(8,128)(2,1)S(1)} collective-permute-done((bf16[8,32,1024]{2,1,0:T(8,128)(2,1)S(1)}, bf16[8,32,1024]{2,1,0:T(8,128)(2,1)S(1)}, u32[]{:S(2)}, u32[]{:S(2)}) %collective-permute-start.3) | collective-permute-done | bytes 524320 | tf_op jit(solution)/shard_map/ppermute | solution.py:517
  73.6 3.3 all-to-all-start
  79.9 4.4 %all_gather.3 = f32[2048]{0:T(1024)} all-gather(f32[1024]{0:T(1024)S(1)} %copy-done.18), channel_id=1, replica_groups=mesh['dp'=16,'tensor'=2] {'tensor'}, dimensions={0}, use_global_device_ids=true | all-gather | bytes 12288 | tf_op jit(solution)/shard_map/all_gather | solution.py:591
  86.2 17.6 %attention_forward.1 = (bf16[2048,512]{1,0:T(8,128)(2,1)}, bf16[2048,512]{1,0:T(8,128)(2,1)}, bf16[4,544,512]{2,1,0:T(8,128)(2,1)}, bf16[4,544,512]{2,1,0:T(8,12...) custom-call(s32[6,8]{1,0:T(8,128)} %stack.102.meta, s32[2,32]{1,0:T(2,128)} %pad_add_fusion.1.places, ...), custom_call_target="tpu_custom_call" | custom-call | flops 5637144576 | bytes 14680064 | tf_op jit(solution)/shard_map/attention_forward/pallas_call | solution.py:186
  106.0 43.1 %feed_forward.1 = (bf16[2048,512]{1,0:T(8,128)(2,1)}, bf16[2048,512]{1,0:T(8,128)(2,1)}, bf16[2,512,2176]{2,1,0:T(8,128)(2,1)}, f32[24,512]{1,0:T(8,128)}, f32[8,2048]{1,0:T(8,128)}) custom-call(s32[6,8]{1,0:T(8,128)} %stack.102.meta, s32[2,32]{1,0:T(2,128)} %pad_add_fusion.places, f32[2048,512]{1,0:T(8,128)} %get-tuple-element.44.mid_ref, ...), custom_call_target="tpu_custom_call" | custom-call | flops 25769803776 | bytes 10485760 | tf_op jit(solution)/shard_map/feed_forward/pallas_call | solution.py:303
  149.1 39.2 %attention_backward.1 = (bf16[2048,512]{1,0:T(8,128)(2,1)}, f32[4,16,512]{2,1,0:T(8,128)}, f32[4,16,512]{2,1,0:T(8,128)}, bf16[2,512,1152]{2,1,0:T(8,128)(2,1)}, f32[16,512]{1,0:T(8,128)}) custom-call(s32[6,8]{1,0:T(8,128)} %stack.102.meta, s32[2,32]{1,0:T(2,128)} %pad_add_fusion.1.places, bf16[4096,512]{1,0:T(8,128)(2,1)} %frames_ref.3, ...), custom_call_target="tpu_custom_call" | custom-call | flops 11945377792 | bytes 14680064 | tf_op jit(solution)/shard_map/attention_backward/pallas_call | solution.py:454
  193.1 3.3 constant_dynamic-slice_fusion.4
  201.1 3.7 all-to-all-start.1
  223.9 88.4 %collective-permute-done.13 = bf16[1,2,2,2,1,32,1152]{6,5,4,3,2,1,0:T(8,128)(2,1)} collective-permute-done((bf16[1,2,2,2,1,32,1152]{6,5,4,3,2,1,0:T(8,128)(2,1)}, bf16[1,2,2,2,1,32,1152]{6,5,4,3,2,1,0:T(8,128)(2,1)}, u32[]{:S(2)}, u32[]{:S(2)}) %collective-permute-start.13) | collective-permute-done | bytes 589856 | tf_op jit(solution)/shard_map/ppermute | solution.py:517
  318.8 4.8 %collective-permute-done.14 = bf16[1,2,2,1,1,32,1152]{6,5,4,3,2,1,0:T(8,128)(2,1)S(1)} collective-permute-done((bf16[1,2,2,1,1,32,1152]{6,5,4,3,2,1,0:T(8,128)(2,1)S(1)}, bf16[1,2,2,1,1,32,1152]{6,5,4,3,2,1,0:T(8,128)(2,1)S(1)}, u32[]{:S(2)}, u32[]{:S(2)}) %collective-permute-start.14) | collective-permute-done | bytes 294944 | tf_op jit(solution)/shard_map/ppermute | solution.py:517
  323.7 4.0 %collective-permute-start.15 = (bf16[1,2,1,1,1,32,1152]{6,5,4,3,2,1,0:T(8,128)(2,1)S(1)}, bf16[1,2,1,1,1,32,1152]{6,5,4,3,2,1,0:T(8,128)(2,1)S(1)}, u32[]{:S(2)}, u32[]{:S(2)}) collective-permute-start(bf16[1,2,1,1,1,32,1152]{6,5,4,3,2,1,0:T(8,128)(2,1)S(1)} %constant_dynamic-slice_fusion.6), channel_id=1, source_target_pairs={{0,8},{2,10},{4,12},{6,14},{8,0},{10,2},{12,4},{14,6},{16,24},{18,... | collective-permute-start | bytes 442376 | tf_op jit(solution)/shard_map/ppermute | solution.py:517
  329.5 4.6 %constant_dynamic-update-slice_fusion.26 = bf16[4096,512]{1,0:T(8,128)(2,1)} fusion(bf16[4096,512]{1,0:T(8,128)(2,1)} %constant_dynamic-update-slice_fusion.27, bf16[2048,512]{1,0:T(8,128)(2,1)} %collective-permute-done.10, s32[]{:T(128)S(6)} %select_n.109), kind=kLoop, calls=%fused_computation.84 | loop fusion | bytes 4194308 | tf_op jit(solution)/shard_map/dynamic_update_slice | solution.py:640
  334.0 12.0 %collective-permute-done.18 = bf16[2,2,2,1,1,32,2176]{6,5,4,3,2,1,0:T(8,128)(2,1)S(1)} collective-permute-done((bf16[2,2,2,1,1,32,2176]{6,5,4,3,2,1,0:T(8,128)(2,1)S(1)}, bf16[2,2,2,1,1,32,2176]{6,5,4,3,2,1,0:T(8,128)(2,1)S(1)}, u32[]{:S(2)}, u32[]{:S(2)}) %collective-permute-start.18) | collective-permute-done | bytes 1114144 | tf_op jit(solution)/shard_map/ppermute | solution.py:517
  346.5 4.0 %collective-permute-start.19 = (bf16[2,2,1,1,1,32,2176]{6,5,4,3,2,1,0:T(8,128)(2,1)S(1)}, bf16[2,2,1,1,1,32,2176]{6,5,4,3,2,1,0:T(8,128)(2,1)S(1)}, u32[]{:S(2)}, u32[]{:S(2)}) collective-permute-start(bf16[2,2,1,1,1,32,2176]{6,5,4,3,2,1,0:T(8,128)(2,1)S(1)} %constant_dynamic-slice_fusion.2), channel_id=1, source_target_pairs={{0,8},{2,10},{4,12},{6,14},{8,0},{10,2},{12,4},{14,6},{16,24},{18,... | collective-permute-start | bytes 1671176 | tf_op jit(solution)/shard_map/ppermute | solution.py:517
  350.5 3.4 collective-permute-start.16
  354.0 9.6 %collective-permute-done.19 = bf16[2,2,1,1,1,32,2176]{6,5,4,3,2,1,0:T(8,128)(2,1)S(1)} collective-permute-done((bf16[2,2,1,1,1,32,2176]{6,5,4,3,2,1,0:T(8,128)(2,1)S(1)}, bf16[2,2,1,1,1,32,2176]{6,5,4,3,2,1,0:T(8,128)(2,1)S(1)}, u32[]{:S(2)}, u32[]{:S(2)}) %collective-permute-start.19) | collective-permute-done | bytes 557088 | tf_op jit(solution)/shard_map/ppermute | solution.py:517
  363.7 3.6 collective-permute-start.20
  368.0 10.1 %collective-permute-done.20 = bf16[2,1,1,1,1,32,2176]{6,5,4,3,2,1,0:T(8,128)(2,1)S(1)} collective-permute-done((bf16[2,1,1,1,1,32,2176]{6,5,4,3,2,1,0:T(8,128)(2,1)S(1)}, bf16[2,1,1,1,1,32,2176]{6,5,4,3,2,1,0:T(8,128)(2,1)S(1)}, u32[]{:S(2)}, u32[]{:S(2)}) %collective-permute-start.20) | collective-permute-done | bytes 278560 | tf_op jit(solution)/shard_map/ppermute | solution.py:517
  378.9 4.5 %collective-permute-done.21 = bf16[1,1,1,1,1,32,2176]{6,5,4,3,2,1,0:T(8,128)(2,1)S(1)} collective-permute-done((bf16[1,1,1,1,1,32,2176]{6,5,4,3,2,1,0:T(8,128)(2,1)S(1)}, bf16[1,1,1,1,1,32,2176]{6,5,4,3,2,1,0:T(8,128)(2,1)S(1)}, u32[]{:S(2)}, u32[]{:S(2)}) %collective-permute-start.21) | collective-permute-done | bytes 139296 | tf_op jit(solution)/shard_map/ppermute | solution.py:517
  (191 shorter events, 70.9 us)
Async XLA Ops:
  1.6 10.4 %collective-permute-start.5 = (bf16[1,32,2048]{2,1,0:T(8,128)(2,1)S(1)}, bf16[1,32,2048]{2,1,0:T(8,128)(2,1)S(1)}, u32[]{:S(2)}, u32[]{:S(2)}) collective-permute-start(bf16[1,32,2048]{2,1,0:T(8,128)(2,1)S(1)} %maximum_bitcast_fusion), channel_id=1, source_target_pairs={{0,16},{2,18},{4,20},{6,22},{8,24},{10,26},{12,28},{14,30},{16,0},... | collective-permute-start | bytes 393224 | tf_op jit(solution)/shard_map/ppermute | solution.py:517
  12.0 7.6 %collective-permute-start.6 = (bf16[2,32,2048]{2,1,0:T(8,128)(2,1)S(1)}, bf16[2,32,2048]{2,1,0:T(8,128)(2,1)S(1)}, u32[]{:S(2)}, u32[]{:S(2)}) collective-permute-start(bf16[2,32,2048]{2,1,0:T(8,128)(2,1)S(1)} %pad_maximum_fusion.5), channel_id=1, source_target_pairs={{0,8},{2,10},{4,12},{6,14},{8,0},{10,2},{12,4},{14,6},{16,24},{18,... | collective-permute-start | bytes 786440 | tf_op jit(solution)/shard_map/ppermute | solution.py:517
  19.6 12.3 %collective-permute-start.7 = (bf16[4,32,2048]{2,1,0:T(8,128)(2,1)S(1)}, bf16[4,32,2048]{2,1,0:T(8,128)(2,1)S(1)}, u32[]{:S(2)}, u32[]{:S(2)}) collective-permute-start(bf16[4,32,2048]{2,1,0:T(8,128)(2,1)S(1)} %pad_maximum_fusion.2), channel_id=1, source_target_pairs={{0,1},{1,0},{2,3},{3,2},{4,5},{5,4},{6,7},{7,6},{8,9},{9,8},{10,11... | collective-permute-start | bytes 1572872 | tf_op jit(solution)/shard_map/ppermute | solution.py:517
  21.7 5.7 %collective-permute-start = (bf16[1,32,1024]{2,1,0:T(8,128)(2,1)S(1)}, bf16[1,32,1024]{2,1,0:T(8,128)(2,1)S(1)}, u32[]{:S(2)}, u32[]{:S(2)}) collective-permute-start(bf16[1,32,1024]{2,1,0:T(8,128)(2,1)S(1)} %maximum_bitcast_fusion.1), channel_id=1, source_target_pairs={{0,16},{2,18},{4,20},{6,22},{8,24},{10,26},{12,28},{14,30},{16,0},... | collective-permute-start | bytes 196616 | tf_op jit(solution)/shard_map/ppermute | solution.py:517
  27.5 6.6 %collective-permute-start.1 = (bf16[2,32,1024]{2,1,0:T(8,128)(2,1)S(1)}, bf16[2,32,1024]{2,1,0:T(8,128)(2,1)S(1)}, u32[]{:S(2)}, u32[]{:S(2)}) collective-permute-start(bf16[2,32,1024]{2,1,0:T(8,128)(2,1)S(1)} %pad_maximum_fusion.6), channel_id=1, source_target_pairs={{0,8},{2,10},{4,12},{6,14},{8,0},{10,2},{12,4},{14,6},{16,24},{18,... | collective-permute-start | bytes 393224 | tf_op jit(solution)/shard_map/ppermute | solution.py:517
  32.0 30.5 %collective-permute-start.8 = (bf16[8,32,2048]{2,1,0:T(8,128)(2,1)S(1)}, bf16[8,32,2048]{2,1,0:T(8,128)(2,1)S(1)}, u32[]{:S(2)}, u32[]{:S(2)}) collective-permute-start(bf16[8,32,2048]{2,1,0:T(8,128)(2,1)S(1)} %pad_maximum_fusion), channel_id=1, source_target_pairs={{0,4},{2,6},{4,0},{6,2},{8,12},{10,14},{12,8},{14,10},{16,20},{18,... | collective-permute-start | bytes 3145736 | tf_op jit(solution)/shard_map/ppermute | solution.py:517
  34.1 26.1 %collective-permute-start.2 = (bf16[4,32,1024]{2,1,0:T(8,128)(2,1)S(1)}, bf16[4,32,1024]{2,1,0:T(8,128)(2,1)S(1)}, u32[]{:S(2)}, u32[]{:S(2)}) collective-permute-start(bf16[4,32,1024]{2,1,0:T(8,128)(2,1)S(1)} %pad_maximum_fusion.4), channel_id=1, source_target_pairs={{0,4},{2,6},{4,0},{6,2},{8,12},{10,14},{12,8},{14,10},{16,20},{18,... | collective-permute-start | bytes 786440 | tf_op jit(solution)/shard_map/ppermute | solution.py:517
  60.3 10.4 %collective-permute-start.3 = (bf16[8,32,1024]{2,1,0:T(8,128)(2,1)S(1)}, bf16[8,32,1024]{2,1,0:T(8,128)(2,1)S(1)}, u32[]{:S(2)}, u32[]{:S(2)}) collective-permute-start(bf16[8,32,1024]{2,1,0:T(8,128)(2,1)S(1)} %pad_maximum_fusion.1), channel_id=1, source_target_pairs={{0,1},{1,0},{2,3},{3,2},{4,5},{5,4},{6,7},{7,6},{8,9},{9,8},{10,11... | collective-permute-start | bytes 1572872 | tf_op jit(solution)/shard_map/ppermute | solution.py:517
  63.8 40.0 %collective-permute-start.9 = (bf16[16,32,2048]{2,1,0:T(8,128)(2,1)}, bf16[16,32,2048]{2,1,0:T(8,128)(2,1)S(1)}, u32[]{:S(2)}, u32[]{:S(2)}) collective-permute-start(bf16[16,32,2048]{2,1,0:T(8,128)(2,1)} %get-tuple-element.65), channel_id=1, source_target_pairs={{0,2},{2,0},{4,6},{6,4},{8,10},{10,8},{12,14},{14,12},{16,18},{18,... | collective-permute-start | bytes 6291464 | tf_op jit(solution)/shard_map/ppermute | solution.py:517
  71.6 13.6 %collective-permute-start.4 = (bf16[16,32,1024]{2,1,0:T(8,128)(2,1)}, bf16[16,32,1024]{2,1,0:T(8,128)(2,1)S(1)}, u32[]{:S(2)}, u32[]{:S(2)}) collective-permute-start(bf16[16,32,1024]{2,1,0:T(8,128)(2,1)} %get-tuple-element.69), channel_id=1, source_target_pairs={{0,2},{2,0},{4,6},{6,4},{8,10},{10,8},{12,14},{14,12},{16,18},{18,... | collective-permute-start | bytes 3145736 | tf_op jit(solution)/shard_map/ppermute | solution.py:517
  73.6 10.7 %all-to-all-start = ((bf16[2,8,10,256]{3,0,2,1:T(2,128)(2,1)}), bf16[2,8,10,256]{3,0,2,1:T(2,128)(2,1)S(1)}, u32[]{:S(2)}, u32[]{:S(2)}) async-start(bf16[2,8,10,256]{3,0,2,1:T(2,128)(2,1)} %copy.64), calls=%async_computation | async-start | bytes 163840 | tf_op jit(solution)/shard_map/all_to_all | solution.py:611
  191.6 15.3 %collective-permute-start.12 = (bf16[2,2,2,2,1,32,1152]{6,5,4,3,2,1,0:T(8,128)(2,1)S(1)}, bf16[2,2,2,2,1,32,1152]{6,5,4,3,2,1,0:T(8,128)(2,1)}, u32[]{:S(2)}, u32[]{:S(2)}) collective-permute-start(bf16[2,2,2,2,1,32,1152]{6,5,4,3,2,1,0:T(8,128)(2,1)S(1)} %constant_dynamic-slice_fusion.9), channel_id=1, source_target_pairs={{0,2},{2,0},{4,6},{6,4},{8,10},{10,8},{12,14},{14,12},{16,18},{18,... | collective-permute-start | bytes 3538952 | tf_op jit(solution)/shard_map/ppermute | solution.py:517
  196.4 118.7 %collective-permute-start.17 = (bf16[2,2,2,2,1,32,2176]{6,5,4,3,2,1,0:T(8,128)(2,1)}, bf16[2,2,2,2,1,32,2176]{6,5,4,3,2,1,0:T(8,128)(2,1)}, u32[]{:S(2)}, u32[]{:S(2)}) collective-permute-start(bf16[2,2,2,2,1,32,2176]{6,5,4,3,2,1,0:T(8,128)(2,1)} %constant_dynamic-slice_fusion.4), channel_id=1, source_target_pairs={{0,2},{2,0},{4,6},{6,4},{8,10},{10,8},{12,14},{14,12},{16,18},{18,... | collective-permute-start | bytes 6684680 | tf_op jit(solution)/shard_map/ppermute | solution.py:517
  201.1 16.0 %all-to-all-start.1 = ((f32[2,1,20480]{2,1,0:T(1,128)}), f32[2,1,20480]{2,1,0:T(1,128)S(1)}, u32[]{:S(2)}, u32[]{:S(2)}) async-start(f32[2,1,20480]{2,1,0:T(1,128)} %reshape.125), calls=%async_computation.1 | async-start | bytes 327680 | tf_op jit(solution)/shard_map/all_to_all | solution.py:645
  204.8 122.9 %collective-permute-start.11 = (bf16[2048,512]{1,0:T(8,128)(2,1)}, bf16[2048,512]{1,0:T(8,128)(2,1)}, u32[]{:S(2)}, u32[]{:S(2)}) collective-permute-start(bf16[2048,512]{1,0:T(8,128)(2,1)} %get-tuple-element.52), channel_id=1, source_target_pairs={{0,1},{1,0},{2,3},{3,2},{4,5},{5,4},{6,7},{7,6},{8,9},{9,8},{10,11... | collective-permute-start | bytes 6291464 | tf_op jit(solution)/shard_map/ppermute | solution.py:517
  206.8 122.7 %collective-permute-start.10 = (bf16[2048,512]{1,0:T(8,128)(2,1)}, bf16[2048,512]{1,0:T(8,128)(2,1)}, u32[]{:S(2)}, u32[]{:S(2)}) collective-permute-start(bf16[2048,512]{1,0:T(8,128)(2,1)} %get-tuple-element.45), channel_id=1, source_target_pairs={{0,1},{1,0},{2,3},{3,2},{4,5},{5,4},{6,7},{7,6},{8,9},{9,8},{10,11... | collective-permute-start | bytes 6291464 | tf_op jit(solution)/shard_map/ppermute | solution.py:517
  209.7 102.6 %collective-permute-start.13 = (bf16[1,2,2,2,1,32,1152]{6,5,4,3,2,1,0:T(8,128)(2,1)}, bf16[1,2,2,2,1,32,1152]{6,5,4,3,2,1,0:T(8,128)(2,1)}, u32[]{:S(2)}, u32[]{:S(2)}) collective-permute-start(bf16[1,2,2,2,1,32,1152]{6,5,4,3,2,1,0:T(8,128)(2,1)} %constant_dynamic-slice_fusion.8), channel_id=1, source_target_pairs={{0,1},{1,0},{2,3},{3,2},{4,5},{5,4},{6,7},{7,6},{8,9},{9,8},{10,11... | collective-permute-start | bytes 1769480 | tf_op jit(solution)/shard_map/ppermute | solution.py:517
  313.6 10.0 %collective-permute-start.14 = (bf16[1,2,2,1,1,32,1152]{6,5,4,3,2,1,0:T(8,128)(2,1)S(1)}, bf16[1,2,2,1,1,32,1152]{6,5,4,3,2,1,0:T(8,128)(2,1)S(1)}, u32[]{:S(2)}, u32[]{:S(2)}) collective-permute-start(bf16[1,2,2,1,1,32,1152]{6,5,4,3,2,1,0:T(8,128)(2,1)S(1)} %constant_dynamic-slice_fusion.7), channel_id=1, source_target_pairs={{0,4},{2,6},{4,0},{6,2},{8,12},{10,14},{12,8},{14,10},{16,20},{18,... | collective-permute-start | bytes 884744 | tf_op jit(solution)/shard_map/ppermute | solution.py:517
  318.1 28.0 %collective-permute-start.18 = (bf16[2,2,2,1,1,32,2176]{6,5,4,3,2,1,0:T(8,128)(2,1)S(1)}, bf16[2,2,2,1,1,32,2176]{6,5,4,3,2,1,0:T(8,128)(2,1)S(1)}, u32[]{:S(2)}, u32[]{:S(2)}) collective-permute-start(bf16[2,2,2,1,1,32,2176]{6,5,4,3,2,1,0:T(8,128)(2,1)S(1)} %constant_dynamic-slice_fusion.3), channel_id=1, source_target_pairs={{0,4},{2,6},{4,0},{6,2},{8,12},{10,14},{12,8},{14,10},{16,20},{18,... | collective-permute-start | bytes 3342344 | tf_op jit(solution)/shard_map/ppermute | solution.py:517
  323.7 26.8 %collective-permute-start.15 = (bf16[1,2,1,1,1,32,1152]{6,5,4,3,2,1,0:T(8,128)(2,1)S(1)}, bf16[1,2,1,1,1,32,1152]{6,5,4,3,2,1,0:T(8,128)(2,1)S(1)}, u32[]{:S(2)}, u32[]{:S(2)}) collective-permute-start(bf16[1,2,1,1,1,32,1152]{6,5,4,3,2,1,0:T(8,128)(2,1)S(1)} %constant_dynamic-slice_fusion.6), channel_id=1, source_target_pairs={{0,8},{2,10},{4,12},{6,14},{8,0},{10,2},{12,4},{14,6},{16,24},{18,... | collective-permute-start | bytes 442376 | tf_op jit(solution)/shard_map/ppermute | solution.py:517
  346.5 17.1 %collective-permute-start.19 = (bf16[2,2,1,1,1,32,2176]{6,5,4,3,2,1,0:T(8,128)(2,1)S(1)}, bf16[2,2,1,1,1,32,2176]{6,5,4,3,2,1,0:T(8,128)(2,1)S(1)}, u32[]{:S(2)}, u32[]{:S(2)}) collective-permute-start(bf16[2,2,1,1,1,32,2176]{6,5,4,3,2,1,0:T(8,128)(2,1)S(1)} %constant_dynamic-slice_fusion.2), channel_id=1, source_target_pairs={{0,8},{2,10},{4,12},{6,14},{8,0},{10,2},{12,4},{14,6},{16,24},{18,... | collective-permute-start | bytes 1671176 | tf_op jit(solution)/shard_map/ppermute | solution.py:517
  350.5 16.8 %collective-permute-start.16 = (bf16[1,1,1,1,1,32,1152]{6,5,4,3,2,1,0:T(8,128)(2,1)S(1)}, bf16[1,1,1,1,1,32,1152]{6,5,4,3,2,1,0:T(8,128)(2,1)S(1)}, u32[]{:S(2)}, u32[]{:S(2)}) collective-permute-start(bf16[1,1,1,1,1,32,1152]{6,5,4,3,2,1,0:T(8,128)(2,1)S(1)} %constant_dynamic-slice_fusion.5), channel_id=1, source_target_pairs={{0,16},{2,18},{4,20},{6,22},{8,24},{10,26},{12,28},{14,30},{16,0},... | collective-permute-start | bytes 221192 | tf_op jit(solution)/shard_map/ppermute | solution.py:517
  363.7 14.4 %collective-permute-start.20 = (bf16[2,1,1,1,1,32,2176]{6,5,4,3,2,1,0:T(8,128)(2,1)S(1)}, bf16[2,1,1,1,1,32,2176]{6,5,4,3,2,1,0:T(8,128)(2,1)S(1)}, u32[]{:S(2)}, u32[]{:S(2)}) collective-permute-start(bf16[2,1,1,1,1,32,2176]{6,5,4,3,2,1,0:T(8,128)(2,1)S(1)} %constant_dynamic-slice_fusion.1), channel_id=1, source_target_pairs={{0,16},{2,18},{4,20},{6,22},{8,24},{10,26},{12,28},{14,30},{16,0},... | collective-permute-start | bytes 835592 | tf_op jit(solution)/shard_map/ppermute | solution.py:517
  378.2 5.1 %collective-permute-start.21 = (bf16[1,1,1,1,1,32,2176]{6,5,4,3,2,1,0:T(8,128)(2,1)S(1)}, bf16[1,1,1,1,1,32,2176]{6,5,4,3,2,1,0:T(8,128)(2,1)S(1)}, u32[]{:S(2)}, u32[]{:S(2)}) collective-permute-start(bf16[1,1,1,1,1,32,2176]{6,5,4,3,2,1,0:T(8,128)(2,1)S(1)} %constant_dynamic-slice_fusion), channel_id=1, source_target_pairs={{0,1},{1,0},{2,3},{3,2},{4,5},{5,4},{6,7},{7,6},{8,9},{9,8},{10,11... | collective-permute-start | bytes 417800 | tf_op jit(solution)/shard_map/ppermute | solution.py:517
  (30 other events, 356.8 us)
